TPU v7x, 512 devices: a whole 4x4x16 slice. The times are simulated.
512 devices in a mesh: sample: 16 (over z_hi, y, core), context: 32 (over z_lo, x).
Axes of the slice: x: 4, y: 4, z: 16 (z_hi: 2, z_lo: 8; z = z_hi * 8 + z_lo), core: 2. Of those that a mesh axis runs over, the one named last changes fastest.
Arguments:
- hidden_in: bfloat16 [3, 32, 16, 4608], P(None, 'context', 'sample'), may hold values from -6 to 6
- pre_gain: bfloat16 [4608], replicated, may hold values from 0.099609375 to 1.8984375
- post_gain: bfloat16 [4608], replicated, may hold values from 0.099609375 to 1.8984375
- w_query: bfloat16 [4608, 4096], P('context', 'sample'), may hold values from -0.09375 to 0.09375
- key_projection_weight: bfloat16 [4608, 2048], P('context', 'sample'), may hold values from -0.09375 to 0.09375
- value_projection_weight: bfloat16 [4608, 2048], P('context', 'sample'), may hold values from -0.09375 to 0.09375
- w_out: bfloat16 [4096, 4608], P('sample'), may hold values from -0.09375 to 0.09375
- prompt_rotated_keys: bfloat16 [32768, 2048], P('context', 'sample'), may hold values from -18 to 18
- prompt_value_rows: bfloat16 [32768, 2048], P('context', 'sample'), may hold values from -6 to 6
- suffix_key_cache: bfloat16 [32, 16, 128, 2048], P('context', None, None, 'sample'), may hold values from -18 to 18
- suffix_value_cache: bfloat16 [32, 16, 128, 2048], P('context', None, None, 'sample'), may hold values from -6 to 6
- parents: int32 [3, 32, 16], P(None, 'context'), may hold values from 0 to 15
- lengths: int32 [32], replicated, may hold values from 1 to 125, as said below
Outputs:
- hidden_out: float32 [3, 32, 16, 4608], P(None, 'context', 'sample')
- keys_out: bfloat16 [32, 16, 128, 2048], P('context', None, None, 'sample')
- values_out: bfloat16 [32, 16, 128, 2048], P('context', None, None, 'sample')
Inputs may be any that keep to these rules, and one draw needn't show every extreme that they name: `lengths`: some request has exactly 125 valid slots. parents[t] refer to the beams as reordered by the earlier steps.
All inputs are finite; a program needn't handle non-finite values.
Results may differ from a plain program's by a relative error of at most 0.012.
Values may be sent and summed in bfloat16 or wider, within the bound.
A program may use at most 64 MiB of HBM per device.

v0:
```python
import jax
import jax.numpy as jnp
from jax import lax
from jax.sharding import PartitionSpec as P

HEAD_SIZE = 128


epsilon = 1e-06
query_scale = 144.0 ** (-0.5)
rope_base = 10000.0
logit_cap = 50.0


def apply_pair_rotation(vectors, decode_position):
    half_dim = vectors.shape[-1] // 2
    frequency = rope_base ** (-2.0 * jnp.arange(half_dim, dtype=jnp.float32) / vectors.shape[-1])
    angles = decode_position.astype(jnp.float32)[..., None, None] * frequency
    cosine = jnp.cos(angles)
    sine = jnp.sin(angles)
    lower_half = vectors[..., :half_dim]
    upper_half = vectors[..., half_dim:]
    return jnp.concatenate(
        [lower_half * cosine - upper_half * sine, upper_half * cosine + lower_half * sine], axis=-1
    )


def soft_cap(scores):
    return logit_cap * jnp.tanh(scores / logit_cap)


def body(
    hidden_in,
    pre_gain,
    post_gain,
    w_query,
    key_projection_weight,
    value_projection_weight,
    w_out,
    prompt_rotated_keys,
    prompt_value_rows,
    suffix_key_cache,
    suffix_value_cache,
    parents,
    lengths,
):
    step_count = hidden_in.shape[0]
    req_dev = hidden_in.shape[1]
    context_size = lax.axis_size("context")
    context_at = lax.axis_index("context")
    my_start = context_at * req_dev
    head_dim = HEAD_SIZE
    query_width = w_query.shape[1]
    key_width = key_projection_weight.shape[1]
    kv_local = key_width // head_dim
    query_group_width = query_width // key_width
    beam_count = suffix_key_cache.shape[1]
    slot_count = suffix_key_cache.shape[2]
    prefix_local = prompt_rotated_keys.shape[0]
    prefix_total = prefix_local * context_size
    w_joint = jnp.concatenate([w_query, key_projection_weight, value_projection_weight], axis=1)
    my_lengths = lax.dynamic_slice_in_dim(lengths, my_start, req_dev)
    keys_prefix = prompt_rotated_keys.reshape(prefix_local, kv_local, head_dim)
    values_prefix = prompt_value_rows.reshape(prefix_local, kv_local, head_dim)
    keys_cache = suffix_key_cache
    values_cache = suffix_value_cache
    slot_index = jnp.arange(slot_count, dtype=jnp.int32)
    suffix_cache_shape = (req_dev, beam_count, slot_count, kv_local, head_dim)
    results = []
    for step_index in range(step_count):
        rows_float = hidden_in[step_index].astype(jnp.float32)
        mean_square = jnp.mean(rows_float * rows_float, axis=-1, keepdims=True)
        normed = (
            rows_float * lax.rsqrt(mean_square + epsilon) * pre_gain.astype(jnp.float32)
        ).astype(jnp.bfloat16)
        spread = lax.all_to_all(normed, "context", split_axis=2, concat_axis=0, tiled=True)
        partial_sums = jnp.einsum(
            "rbd,dc->rbc",
            lax.all_gather(spread, "sample", axis=1, tiled=True),
            w_joint,
            preferred_element_type=jnp.float32,
        )
        summed = lax.psum(partial_sums, "context")
        row_total = summed.shape[0]
        decode_position = (prefix_total + lengths + step_index)[:, None]
        query_part = summed[..., :query_width].reshape(
            row_total, beam_count, query_width // head_dim, head_dim
        )
        query_rows = (apply_pair_rotation(query_part, decode_position) * query_scale).astype(
            jnp.bfloat16
        )
        query_rows = query_rows.reshape(
            row_total, beam_count, kv_local, query_group_width, head_dim
        )
        key_part = summed[..., query_width : query_width + key_width].reshape(
            row_total, beam_count, kv_local, head_dim
        )
        fresh_rotated_keys = (
            apply_pair_rotation(key_part, decode_position)
            .astype(jnp.bfloat16)
            .reshape(row_total, beam_count, key_width)
        )
        new_values = summed[..., query_width + key_width :].astype(jnp.bfloat16)
        all_keys = fresh_rotated_keys
        all_values = new_values
        my_queries = lax.dynamic_slice_in_dim(query_rows, my_start, req_dev, 0)
        fresh_rotated_keys = lax.dynamic_slice_in_dim(all_keys, my_start, req_dev, 0)
        new_values = lax.dynamic_slice_in_dim(all_values, my_start, req_dev, 0)
        scores = jnp.einsum(
            "rbgeh,pgh->rbgep", query_rows, keys_prefix, preferred_element_type=jnp.float32
        )
        weights = jnp.exp(soft_cap(scores))
        weighted = jnp.einsum(
            "rbgep,pgh->rbgeh",
            weights.astype(jnp.bfloat16),
            values_prefix,
            preferred_element_type=jnp.float32,
        )
        totals = jnp.sum(weights, axis=-1)
        prefix_weighted, prefix_totals = (
            lax.psum_scatter(weighted, "context", scatter_dimension=0, tiled=True),
            lax.psum_scatter(totals, "context", scatter_dimension=0, tiled=True),
        )
        ancestors = parents[step_index][:, :, None, None]
        keys_cache = jnp.take_along_axis(keys_cache, ancestors, axis=1)
        values_cache = jnp.take_along_axis(values_cache, ancestors, axis=1)
        write_slot = my_lengths + step_index
        at_slot = (slot_index[None, :] == write_slot[:, None])[:, None, :, None]
        keys_cache = jnp.where(at_slot, fresh_rotated_keys[:, :, None, :], keys_cache)
        values_cache = jnp.where(at_slot, new_values[:, :, None, :], values_cache)
        suffix_scores = jnp.einsum(
            "rbgeh,rbjgh->rbgej",
            my_queries,
            keys_cache.reshape(suffix_cache_shape),
            preferred_element_type=jnp.float32,
        )
        visible = (slot_index[None, :] <= write_slot[:, None])[:, None, None, None, :]
        suffix_weights = jnp.where(visible, jnp.exp(soft_cap(suffix_scores)), 0.0)
        suffix_weighted = jnp.einsum(
            "rbgej,rbjgh->rbgeh",
            suffix_weights.astype(jnp.bfloat16),
            values_cache.reshape(suffix_cache_shape),
            preferred_element_type=jnp.float32,
        )
        suffix_totals = jnp.sum(suffix_weights, axis=-1)
        attended = (
            (prefix_weighted + suffix_weighted) / (prefix_totals + suffix_totals)[..., None]
        ).astype(jnp.bfloat16)
        attended = jnp.swapaxes(attended.reshape(req_dev, beam_count, query_width), 0, 1)
        branch = lax.psum_scatter(
            jnp.einsum("brq,qd->brd", attended, w_out, preferred_element_type=jnp.float32),
            "sample",
            scatter_dimension=0,
            tiled=True,
        )
        branch = jnp.swapaxes(branch, 0, 1)
        branch_square = jnp.mean(branch * branch, axis=-1, keepdims=True)
        scaled = branch * lax.rsqrt(branch_square + epsilon) * post_gain.astype(jnp.float32)
        results.append(rows_float + scaled)
    return (jnp.stack(results), keys_cache, values_cache)


def solution(mesh):
    placed = (
        P(None, "context", "sample", None),
        P(),
        P(),
        P("context", "sample"),
        P("context", "sample"),
        P("context", "sample"),
        P("sample", None),
        P("context", "sample"),
        P("context", "sample"),
        P("context", None, None, "sample"),
        P("context", None, None, "sample"),
        P(None, "context", None),
        P(),
    )
    return jax.shard_map(
        body,
        mesh=mesh,
        in_specs=placed,
        out_specs=(
            P(None, "context", "sample", None),
            P("context", None, None, "sample"),
            P("context", None, None, "sample"),
        ),
        check_vma=False,
    )
```

profile of v0, /device:TPU:1, one launch (start us, length us, event | category | flops | bytes accessed | tf_op | source)
XLA Modules:
  0.0 1991.6 jit_solution(10177822948233651296)
XLA Ops:
  12.7 16.1 convert_element_type.214
  28.8 16.0 all-to-all-start.1
  44.8 16.1 convert_element_type.215
  60.9 16.1 convert_element_type.213
  77.0 73.9 %all-to-all-done.1 = bf16[1,1,4608]{1,0,2:T(2,128)(2,1)} async-done(((bf16[1,1,4608]{1,0,2:T(2,128)(2,1)}), bf16[1,1,4608]{1,0,2:T(2,128)(2,1)}, u32[]{:S(2)}, u32[]{:S(2)}) %all-to-all-start.1) | async-done | bytes 9248 | tf_op jit(solution)/shard_map/all_to_all | solution.py:76
  150.9 8.3 all-to-all-start.2
  159.2 35.4 %reduce.18 = bf16[4608]{0:T(1024)(128)(2,1)S(1)} reduce(bf16[1,1,4608]{1,0,2:T(2,128)(2,1)} %all-to-all-done.1, bf16[]{:T(256)} %constant.108), dimensions={0,1}, to_apply=%all_to_all.14.reduce_sub_computation | reduce | bytes 18434 | tf_op jit(solution)/shard_map/all_to_all | solution.py:76
  194.6 44.5 %all_gather.10 = bf16[32,16,144]{2,0,1:T(8,128)(2,1)S(1)} all-gather(bf16[32,1,144]{2,0,1:T(8,128)(2,1)S(1)} %all_to_all.30), channel_id=1, replica_groups=mesh['sample'=16,'context'=32] {'sample'}, dimensions={1}, use_global_device_ids=true | all-gather | bytes 156672 | tf_op jit(solution)/shard_map/all_gather | solution.py:79
  239.1 29.5 %all-to-all-done.2 = bf16[1,1,4608]{1,0,2:T(2,128)(2,1)} async-done(((bf16[1,1,4608]{1,0,2:T(2,128)(2,1)}), bf16[1,1,4608]{1,0,2:T(2,128)(2,1)}, u32[]{:S(2)}, u32[]{:S(2)}) %all-to-all-start.2) | async-done | bytes 9248 | tf_op jit(solution)/shard_map/all_to_all | solution.py:76
  268.6 32.1 %all-to-all-start = ((bf16[1,1,4608]{1,0,2:T(2,128)(2,1)}), bf16[1,1,4608]{1,0,2:T(2,128)(2,1)}, u32[]{:S(2)}, u32[]{:S(2)}) async-start(bf16[1,1,4608]{1,0,2:T(2,128)(2,1)} %convert_element_type.213), calls=%async_computation | async-start | bytes 4718592 | tf_op jit(solution)/shard_map/all_to_all | solution.py:76
  301.2 35.4 %reduce.20 = bf16[4608]{0:T(1024)(128)(2,1)S(1)} reduce(bf16[1,1,4608]{1,0,2:T(2,128)(2,1)} %all-to-all-done.2, bf16[]{:T(256)} %constant.108), dimensions={0,1}, to_apply=%all_to_all.31.reduce_sub_computation | reduce | bytes 18434 | tf_op jit(solution)/shard_map/all_to_all | solution.py:76
  336.7 42.5 %all_gather.11 = bf16[32,16,144]{2,0,1:T(8,128)(2,1)S(1)} all-gather(bf16[32,1,144]{2,0,1:T(8,128)(2,1)S(1)} %all_to_all.32), channel_id=1, replica_groups=mesh['sample'=16,'context'=32] {'sample'}, dimensions={1}, use_global_device_ids=true | all-gather | bytes 156672 | tf_op jit(solution)/shard_map/all_gather | solution.py:79
  381.8 29.8 %all-to-all-done = bf16[1,1,4608]{1,0,2:T(2,128)(2,1)} async-done(((bf16[1,1,4608]{1,0,2:T(2,128)(2,1)}), bf16[1,1,4608]{1,0,2:T(2,128)(2,1)}, u32[]{:S(2)}, u32[]{:S(2)}) %all-to-all-start) | async-done | bytes 9248 | tf_op jit(solution)/shard_map/all_to_all | solution.py:76
  411.6 35.3 %reduce.16 = bf16[4608]{0:T(1024)(128)(2,1)S(1)} reduce(bf16[1,1,4608]{1,0,2:T(2,128)(2,1)} %all-to-all-done, bf16[]{:T(256)} %constant.108), dimensions={0,1}, to_apply=%all_to_all.12.reduce_sub_computation | reduce | bytes 18434 | tf_op jit(solution)/shard_map/all_to_all | solution.py:76
  447.0 35.5 %all_gather.9 = bf16[32,16,144]{2,0,1:T(8,128)(2,1)S(1)} all-gather(bf16[32,1,144]{2,0,1:T(8,128)(2,1)S(1)} %all_to_all.13), channel_id=1, replica_groups=mesh['sample'=16,'context'=32] {'sample'}, dimensions={1}, use_global_device_ids=true | all-gather | bytes 156672 | tf_op jit(solution)/shard_map/all_gather | solution.py:79
  492.8 450.5 %all-reduce.12.cloned.1.call-done = (f32[32,16,512]{2,1,0:T(8,128)}, f32[32,16,512]{2,1,0:T(8,128)}, f32[32,16,512]{2,1,0:T(8,128)}) async-done(((f32[32,16,512]{2,1,0:T(8,128)}, f32[32,16,512]{2,1,0:T(8,128)}, f32[32,16,512]{2,1,0:T(8,128)}), (f32[32,16,512]{2,1,0:T(8,128)}, f32[32,16,512]{2,1,0:T(8,128)}, f32[32,16,512]{2,1,0:T(8,128)})) %all-reduce.12.cloned.1.call-update) | async-done | bytes 3145744 | tf_op jit(solution)/shard_map/psum | solution.py:83
  989.4 3.0 fusion.9
  994.2 3.8 bitcast_reduce_fusion
  1000.1 207.7 %all-reduce.6 = (f32[32,16,1,2]{1,3,2,0:T(2,128)}, f32[32,16,1,2]{1,3,2,0:T(2,128)}, f32[32,16,1,2]{1,3,2,0:T(2,128)}) all-reduce(f32[32,16,1,2]{1,3,2,0:T(2,128)} %bitcast.321, f32[32,16,1,2]{1,3,2,0:T(2,128)S(1)} %bitcast.320, f32[32,16,1,2]{1,3,2,0:T(2,128)S(1)} %bitcast.319), channel_id=9, replica_groups=mesh['sample'=16,'context'=32] {'context'}, use_global_device_ids=true, to_apply=%region_20.22.clone | all-reduce | flops 3072 | bytes 24576
  1210.9 4.3 fusion.15
  1216.6 9.8 reduce-scatter.7.cloned.1.call-done
  1227.2 233.3 %reduce-scatter.9.cloned.1.call-done = f32[1,16,1,2,128]{4,1,3,0,2:T(8,128)} async-done(((f32[32,16,1,2,128]{4,1,3,0,2:T(8,128)}), f32[1,16,1,2,128]{4,1,3,0,2:T(8,128)}) %reduce-scatter.9.cloned.1.call-update) | async-done | bytes 16400 | tf_op jit(solution)/shard_map/reduce_scatter | solution.py:121
  1463.7 231.2 %reduce-scatter.11.cloned.1.call-done = f32[1,16,1,2,128]{4,1,3,0,2:T(8,128)} async-done(((f32[32,16,1,2,128]{4,1,3,0,2:T(8,128)}), f32[1,16,1,2,128]{4,1,3,0,2:T(8,128)}) %reduce-scatter.11.cloned.1.call-update) | async-done | bytes 16400 | tf_op jit(solution)/shard_map/reduce_scatter | solution.py:121
  1698.1 275.1 %all-reduce.14.cloned.1.call-done = (f32[16,1,4608]{2,0,1:T(8,128)}, f32[16,1,4608]{2,0,1:T(8,128)}, f32[16,1,4608]{2,0,1:T(8,128)}) async-done(((f32[16,1,4608]{2,0,1:T(8,128)}, f32[16,1,4608]{2,0,1:T(8,128)}, f32[16,1,4608]{2,0,1:T(8,128)}), (f32[16,1,4608]{2,0,1:T(8,128)}, f32[16,1,4608]{2,0,1:T(8,128)}, f32[16,1,4608]{2,0,1:T(8,128)})) %all-reduce.14.cloned.1.call-update) | async-done | bytes 884752
  (149 shorter events, 86.6 us)
Async XLA Ops:
  7.2 1454.1 %copy-start = (bf16[256,4608]{1,0:T(8,128)(2,1)S(1)}, bf16[256,4608]{1,0:T(8,128)(2,1)}, u32[]{:S(2)}) copy-start(bf16[256,4608]{1,0:T(8,128)(2,1)} %param.21) | copy-start | bytes 7077892
  28.8 122.1 %all-to-all-start.1 = ((bf16[1,1,4608]{1,0,2:T(2,128)(2,1)}), bf16[1,1,4608]{1,0,2:T(2,128)(2,1)}, u32[]{:S(2)}, u32[]{:S(2)}) async-start(bf16[1,1,4608]{1,0,2:T(2,128)(2,1)} %convert_element_type.214), calls=%async_computation.2 | async-start | bytes 4718592 | tf_op jit(solution)/shard_map/all_to_all | solution.py:76
  150.9 117.8 %all-to-all-start.2 = ((bf16[1,1,4608]{1,0,2:T(2,128)(2,1)}), bf16[1,1,4608]{1,0,2:T(2,128)(2,1)}, u32[]{:S(2)}, u32[]{:S(2)}) async-start(bf16[1,1,4608]{1,0,2:T(2,128)(2,1)} %convert_element_type.215), calls=%async_computation.4 | async-start | bytes 4718592 | tf_op jit(solution)/shard_map/all_to_all | solution.py:76
  194.5 184.6 %copy-start.11 = (bf16[144,256]{1,0:T(8,128)(2,1)S(1)}, bf16[144,256]{1,0:T(8,128)(2,1)}, u32[]{:S(2)}) copy-start(bf16[144,256]{1,0:T(8,128)(2,1)} %param.18) | copy-start | bytes 221188
  194.5 184.6 %copy-start.13 = (bf16[144,128]{1,0:T(8,128)(2,1)S(1)}, bf16[144,128]{1,0:T(8,128)(2,1)}, u32[]{:S(2)}) copy-start(bf16[144,128]{1,0:T(8,128)(2,1)} %param.20) | copy-start | bytes 110596
  194.5 184.6 %copy-start.14 = (bf16[144,128]{1,0:T(8,128)(2,1)S(1)}, bf16[144,128]{1,0:T(8,128)(2,1)}, u32[]{:S(2)}) copy-start(bf16[144,128]{1,0:T(8,128)(2,1)} %param.19) | copy-start | bytes 110596
  268.6 143.0 %all-to-all-start = ((bf16[1,1,4608]{1,0,2:T(2,128)(2,1)}), bf16[1,1,4608]{1,0,2:T(2,128)(2,1)}, u32[]{:S(2)}, u32[]{:S(2)}) async-start(bf16[1,1,4608]{1,0,2:T(2,128)(2,1)} %convert_element_type.213), calls=%async_computation | async-start | bytes 4718592 | tf_op jit(solution)/shard_map/all_to_all | solution.py:76
  300.7 642.5 %all-reduce.12.cloned.1.call-start = ((), (), s32[]{:S(2)}) async-start(), calls=%async_computation.9 | async-start | bytes 6291456 | tf_op jit(solution)/shard_map/psum | solution.py:83
  380.5 103.6 %copy-start.21 = (s32[32]{0:T(128)S(1)}, s32[32]{0:T(128)}, u32[]{:S(2)}) copy-start(s32[32]{0:T(128)} %param.27) | copy-start | bytes 388
  380.5 105.5 %copy-start.20 = (s32[3,1,16]{2,1,0:T(1,128)S(1)}, s32[3,1,16]{2,1,0:T(1,128)}, u32[]{:S(2)}) copy-start(s32[3,1,16]{2,1,0:T(1,128)} %param.26) | copy-start | bytes 580
  380.5 105.6 %copy-start.12 = (bf16[1,16,128,128]{3,2,1,0:T(8,128)(2,1)S(1)}, bf16[1,16,128,128]{3,2,1,0:T(8,128)(2,1)}, u32[]{:S(2)}) copy-start(bf16[1,16,128,128]{3,2,1,0:T(8,128)(2,1)} %param.25) | copy-start | bytes 1572868
  483.9 742.5 %reduce-scatter.7.cloned.1.call-start = ((), (), s32[]{:S(2)}) async-start(), calls=%async_computation.6 | async-start | bytes 540672 | tf_op jit(solution)/shard_map/reduce_scatter | solution.py:121
  943.2 9.6 copy-start.9
  979.8 6.6 copy-start.3
  989.3 3.4 copy-start.18
  989.4 3.4 copy-start.22
  992.4 468.1 %reduce-scatter.9.cloned.1.call-start = ((), (), s32[]{:S(2)}) async-start(), calls=%async_computation.7 | async-start | bytes 540672 | tf_op jit(solution)/shard_map/reduce_scatter | solution.py:121
  992.7 5.2 copy-start.23
  997.9 212.5 %copy-start.2 = (bf16[16,128,128]{2,1,0:T(8,128)(2,1)S(1)}, bf16[16,128,128]{2,1,0:T(8,128)(2,1)}, u32[]{:S(2)}) copy-start(bf16[16,128,128]{2,1,0:T(8,128)(2,1)} %copy-done.1) | copy-start | bytes 1572868
  997.9 212.8 %copy-start.6 = (bf16[1,16,128,128]{3,2,1,0:T(8,128)(2,1)S(1)}, bf16[1,16,128,128]{3,2,1,0:T(8,128)(2,1)}, u32[]{:S(2)}) copy-start(bf16[1,16,128,128]{3,2,1,0:T(8,128)(2,1)} %get-tuple-element.50) | copy-start | bytes 1572868
  1000.0 694.9 %reduce-scatter.11.cloned.1.call-start = ((), (), s32[]{:S(2)}) async-start(), calls=%async_computation.8 | async-start | bytes 540672 | tf_op jit(solution)/shard_map/reduce_scatter | solution.py:121
  1215.2 758.0 %all-reduce.14.cloned.1.call-start = ((), (), s32[]{:S(2)}) async-start(), calls=%async_computation.10 | async-start | bytes 1769472
  1461.3 236.8 %copy-start.19 = (bf16[4608]{0:T(1024)(128)(2,1)S(1)}, bf16[4608]{0:T(1024)(128)(2,1)}, u32[]{:S(2)}) copy-start(bf16[4608]{0:T(1024)(128)(2,1)} %param.17) | copy-start | bytes 27652
  1461.3 521.0 %copy-start.10 = (bf16[3,1,1,4608]{3,0,2,1:T(4,128)(2,1)S(1)}, bf16[3,1,1,4608]{3,0,2,1:T(4,128)(2,1)}, u32[]{:S(2)}) copy-start(bf16[3,1,1,4608]{3,0,2,1:T(4,128)(2,1)} %param.15) | copy-start | bytes 82948
  (8 other events, 15.8 us)
Sparse Core Ops, SparseCore 0:
  484.0 459.1 all-reduce.11
  992.6 233.7 reduce-scatter.6
  1229.2 231.2 reduce-scatter.8
  1463.4 231.4 reduce-scatter.10
  1697.9 275.3 all-reduce.13
where the time goes:
time: 2000 us; the launch traced here: 1990 us
  waiting for transfers between devices  1330 us (66%)
  blocking collectives  330 us (16%)
  other arithmetic  138 us (7%)
  local copies, waits for them, and re-layouts  84.7 us (4%)
  starting transfers between devices  57.5 us (3%)
  matrix products  28.5 us (1%)
  between operations  20 us (1%)
    reduce_scatter x3, waiting for transfers between devices, body(): lax.psum_scatter(weighted, 'context', scatter_dimension=0, tiled=True)  474 us
    psum x1, waiting for transfers between devices, body(): summed = lax.psum(partial_sums, 'context')  450 us
    unnamed x6, waiting for transfers between devices  275 us
    unnamed x1, blocking collectives  208 us
    all_to_all x3, waiting for transfers between devices, body(): lax.all_to_all(normed, 'context', split_axis=2, concat_axis=0, tiled=True)  133 us
    all_gather x3, blocking collectives, body(): lax.all_gather(spread, 'sample', axis=1, tiled=True)  122 us
    all_to_all x3, other arithmetic, body(): lax.all_to_all(normed, 'context', split_axis=2, concat_axis=0, tiled=True)  106 us
    all_to_all x3, starting transfers between devices, body(): lax.all_to_all(normed, 'context', split_axis=2, concat_axis=0, tiled=True)  56.4 us
  transfers between devices with their start and end apart: 8, of which 8 were waited for; matrix products, arithmetic and copies ran while one was open for 7% of the time, Pallas kernels for 0%

commit v1 on v0

v1 whole, which is shorter than its diff:
```python
import functools

import jax
import jax.numpy as jnp
import numpy as np
from jax import lax
from jax.experimental import pallas as pl
from jax.experimental.pallas import tpu as pltpu
from jax.sharding import PartitionSpec as P

HEAD = 128
STEPS = 3
XN = 4
POS_TILE = 512

epsilon = 1e-06
query_scale = 144.0 ** (-0.5)
rope_base = 10000.0
logit_cap = 50.0
MESH = pl.DeviceIdType.MESH
F32 = jnp.float32
BF16 = jnp.bfloat16


def weights_of(scores):
    return jnp.exp(logit_cap * jnp.tanh(scores * (1.0 / logit_cap)))


def dot_t(a, b):
    return lax.dot_general(a, b, (((1,), (1,)), ((), ())), preferred_element_type=F32)


def dot(a, b):
    return jnp.dot(a, b, preferred_element_type=F32)


def kernel(
    dims, prompt_total,
    tiles, hid, gain, cos_rows, sin_rows, perm, wq, wk, wv, wout, pk, pv, kc, vc, par, lens,
    out_h, out_k, out_v,
    a1, a1f, xb, wf, wp, yf, sred, rred, g, gf, qa, kall, vall, acc, psend, precv,
    woutv, kcv, vcv, ancv, freshv, freshk, br, csend, crecv, s1, ysend, yrecv, zsend, zrecv,
    as_, ar, ws, wr, ks, kr, xs, xr, ys, yr, cs, cr, rs, rr, gs, gr, qs, qr, ps, pr,
    bcs, bcr, bys, byr, bzs, bzr, ls,
):
    ZH, YN, KN, ZL = dims
    ZN = ZH * ZL
    YK = YN * KN
    BEAMS = ZH * YK
    ROWS = STEPS * BEAMS
    s = lax.axis_index("sample")
    c = lax.axis_index("context")
    zh = lax.div(s, YK)
    y = lax.div(lax.rem(s, YK), KN)
    k = lax.rem(s, KN)
    zl = lax.div(c, XN)
    x = lax.rem(c, XN)
    z = zh * ZL + zl
    width = hid.shape[1]

    def at(zh_=None, y_=None, k_=None, zl_=None, x_=None):
        zh_ = zh if zh_ is None else zh_
        y_ = y if y_ is None else y_
        k_ = k if k_ is None else k_
        zl_ = zl if zl_ is None else zl_
        x_ = x if x_ is None else x_
        return {"sample": zh_ * YK + y_ * KN + k_, "context": zl_ * XN + x_}

    def rc(src, dst, ssem, rsem, where):
        return pltpu.make_async_remote_copy(
            src_ref=src, dst_ref=dst, send_sem=ssem, recv_sem=rsem,
            device_id=where, device_id_type=MESH,
        )

    def z_at(o):
        zz = lax.rem(z + o, ZN)
        return at(zh_=lax.div(zz, ZL), zl_=lax.rem(zz, ZL)), lax.rem(zz, ZL)

    peers = [z_at(o)[0] for o in range(1, ZN)]
    peers += [at(x_=lax.rem(x + o, XN)) for o in range(1, XN)]
    peers += [at(y_=lax.rem(y + o, YN)) for o in range(1, YN)]
    if KN > 1:
        peers += [at(k_=1 - k)]
    barrier = pltpu.get_barrier_semaphore()
    for peer in peers:
        pl.semaphore_signal(barrier, inc=1, device_id=peer, device_id_type=MESH)
    pl.semaphore_wait(barrier, len(peers))

    a_copies = []
    for o in range(1, ZN):
        where, zl_to = z_at(o)
        cp = rc(tiles.at[zl_to], a1.at[z], as_.at[o], ar.at[o], where)
        cp.start()
        a_copies.append(cp)

    half = wq.shape[1] // 2
    w_src = [wq.at[:, pl.ds(0, half)], wq.at[:, pl.ds(half, half)], wk, wv]

    def w_copy(to):
        return rc(w_src[to], wf.at[x], ws.at[to], wr.at[x], at(x_=to))

    def w_local(to):
        return pltpu.make_async_copy(w_src[to], wf.at[x], ls.at[0])

    for to in range(XN):
        @pl.when(x != to)
        def _():
            w_copy(to).start()

        @pl.when(x == to)
        def _():
            w_local(to).start()

    loc = [
        pltpu.make_async_copy(wout, woutv, ls.at[1]),
        pltpu.make_async_copy(kc, kcv, ls.at[2]),
        pltpu.make_async_copy(vc, vcv, ls.at[3]),
        pltpu.make_async_copy(pk, kall.at[x], ls.at[4]),
        pltpu.make_async_copy(pv, vall.at[x], ls.at[5]),
    ]
    for cp in loc:
        cp.start()

    a1[z] = tiles[zl]
    for cp in a_copies:
        cp.wait_recv()

    TJ = a1.shape[1]
    J = xb.shape[2] // 128
    for i in range(ZN):
        a1f[pl.ds(i * TJ, TJ), :] = a1[i].astype(F32)
    b_own = (x * YN + y) * KN + k
    for t in range(STEPS):
        for j in range(J):
            xb[b_own, pl.ds(t * ZN, ZN), pl.ds(j * 128, 128)] = a1f[
                pl.ds(t * J + j, ZN, stride=TJ), :
            ].astype(BF16)

    def blk(x_, y_, k_):
        return xb.at[(x_ * YN + y_) * KN + k_]

    sends = []

    def push(cp):
        cp.start()
        sends.append(cp)
        return cp

    x_copies = {}
    for o in (1, 3, 2):
        x_copies[o] = push(rc(blk(x, y, k), blk(x, y, k), xs.at[o], xr.at[o], at(x_=lax.rem(x + o, XN))))
    y_copies = {}
    c_copies = {}

    def from_x(ox):
        xo = lax.rem(x + XN - ox, XN)
        for oy in range(1, YN):
            y_copies[ox, oy] = push(
                rc(blk(xo, y, k), blk(xo, y, k), ys.at[ox, oy], yr.at[ox, oy], at(y_=lax.rem(y + oy, YN)))
            )
        to_core(ox, 0)

    def to_core(ox, oy):
        if KN == 1:
            return
        xo = lax.rem(x + XN - ox, XN)
        yo = lax.rem(y + YN - oy, YN)
        c_copies[ox, oy] = push(
            rc(blk(xo, yo, k), blk(xo, yo, k), cs.at[ox, oy], cr.at[ox, oy], at(k_=1 - k))
        )

    from_x(0)
    X_ORDER = (1, 3, 2)
    for ox in X_ORDER:
        x_copies[ox].wait_recv()
        from_x(ox)

    kv_copies = []
    for o in range(1, XN):
        to = at(x_=lax.rem(x + o, XN))
        kv_copies.append(push(rc(pk, kall.at[x], ks.at[0, o], kr.at[0, o], to)))
        kv_copies.append(push(rc(pv, vall.at[x], ks.at[1, o], kr.at[1, o], to)))

    for to in range(XN):
        @pl.when(x != to)
        def _():
            rc(w_src[to], wf.at[to], ws.at[to], wr.at[to], at(x_=to)).wait_recv()

        @pl.when(x == to)
        def _():
            w_local(to).wait()

    depth = XN * wf.shape[1]
    wp[pl.ds(0, depth), :] = wf[...].reshape(depth, HEAD)
    if wp.shape[0] > depth:
        wp[pl.ds(depth, wp.shape[0] - depth), :] = jnp.zeros((wp.shape[0] - depth, HEAD), BF16)

    GR = YK * STEPS * ZN
    r_copies = {}
    for ox in (0,) + X_ORDER:
        xo = lax.rem(x + XN - ox, XN)
        for oy in range(1, YN):
            y_copies[ox, oy].wait_recv()
            to_core(ox, oy)
        for oy in range(YN):
            if KN > 1:
                c_copies[ox, oy].wait_recv()
        xg = xb[pl.ds(xo * YK, YK)].reshape(GR, xb.shape[2])
        yf[...] = dot(xg, wp[...])
        for o in range(ZL):
            zo = lax.rem(zl + o, ZL)
            for t in range(STEPS):
                piece = jnp.concatenate(
                    [
                        yf[pl.ds(t * ZN + h * ZL + zo, YK, stride=STEPS * ZN), :]
                        for h in range(ZH)
                    ],
                    axis=0,
                )
                sred[ox, o, pl.ds(t * BEAMS, BEAMS), :] = piece.astype(BF16)
            if o > 0:
                r_copies[ox, o] = push(
                    rc(sred.at[ox, o], rred.at[ox, o], rs.at[ox, o], rr.at[ox, o], at(zl_=zo))
                )

    scale = jnp.where(x < 2, query_scale, 1.0).astype(F32)
    g_copies = {}
    for ox in (0,) + X_ORDER:
        xo = lax.rem(x + XN - ox, XN)
        total = sred[ox, 0].astype(F32)
        for o in range(1, ZL):
            r_copies[ox, o].wait_recv()
            total = total + rred[ox, o].astype(F32)
        for t in range(STEPS):
            part = total[t * BEAMS : (t + 1) * BEAMS]
            cosine = cos_rows[pl.ds(xo * STEPS + t, 1), :]
            sine = sin_rows[pl.ds(xo * STEPS + t, 1), :]
            turned = part * cosine + pltpu.roll(part, HEAD // 2, 1) * sine
            gf[ox, pl.ds(t * BEAMS, BEAMS), :] = (turned * scale).astype(BF16)
        if ox == 0:
            g[x] = gf[0]
        else:
            g_copies[ox] = push(rc(gf.at[ox], g.at[x], gs.at[ox], gr.at[ox], at(x_=xo)))
    for ox in X_ORDER:
        g_copies[ox].wait_recv()

    q_copies = []
    for o in range(1, ZL):
        q_copies.append(
            push(rc(g.at[pl.ds(0, 2)], qa.at[zl], qs.at[o], qr.at[o], at(zl_=lax.rem(zl + o, ZL))))
        )
    qa[zl] = g[0:2]

    length = lens[c]
    for cp in loc[1:3]:
        cp.wait()
    p0 = [par[0, b] for b in range(BEAMS)]
    p1 = [par[1, b] for b in range(BEAMS)]
    p2 = [par[2, b] for b in range(BEAMS)]
    first_of = [par[0, p1[b]] for b in range(BEAMS)]
    mid_of = [par[1, p2[b]] for b in range(BEAMS)]
    last_of = [par[0, mid_of[b]] for b in range(BEAMS)]
    never = jnp.int32(-1)
    for b in range(BEAMS):
        own = jnp.int32(b)
        chains = (
            (p0[b], own, never, never),
            (first_of[b], p1[b], own + BEAMS, never),
            (last_of[b], mid_of[b], p2[b] + BEAMS, own + 2 * BEAMS),
        )
        for t in range(STEPS):
            row = t * BEAMS + b
            ancv[pl.ds(row, 1), :] = jnp.full((1, 128), chains[t][0], jnp.int32)
            for u in range(STEPS):
                freshv[u, pl.ds(row, 1), :] = jnp.full((1, 128), chains[t][1 + u], jnp.int32)
    my_q = g[0:2].reshape(2 * ROWS, HEAD)
    SLOTS = kcv.shape[1]
    anc = ancv[:, :SLOTS]
    anc2 = jnp.concatenate([anc, anc], axis=0)
    slot = lax.broadcasted_iota(jnp.int32, (2 * ROWS, SLOTS), 1)
    lane = lax.broadcasted_iota(jnp.int32, (ROWS, ROWS), 1)
    seen = (lane == freshv[0, :, :ROWS]) | (lane == freshv[1, :, :ROWS]) | (lane == freshv[2, :, :ROWS])
    seen2 = jnp.concatenate([seen.astype(F32)] * 2, axis=0)
    fresh_w = weights_of(dot_t(my_q, g[2])) * seen2
    suf_w = dot(fresh_w.astype(BF16), g[3])
    suf_t = jnp.sum(fresh_w, axis=1, keepdims=True)
    for b in range(BEAMS):
        cached = weights_of(dot_t(my_q, kcv[b]))
        cached = jnp.where((anc2 == b) & (slot < length), cached, 0.0)
        suf_w = suf_w + dot(cached.astype(BF16), vcv[b])
        suf_t = suf_t + jnp.sum(cached, axis=1, keepdims=True)

    for src, cache, dst in ((2, kcv, out_k), (3, vcv, out_v)):
        freshk[...] = g[src].astype(F32)
        slots = lax.broadcasted_iota(jnp.int32, (SLOTS, HEAD), 0)
        for b in range(BEAMS):
            rows = [
                freshk[pl.ds(mid_of[b], 1), :],
                freshk[pl.ds(p2[b] + BEAMS, 1), :],
                freshk[pl.ds(b + 2 * BEAMS, 1), :],
            ]
            block = cache[last_of[b]].astype(F32)
            for u in range(STEPS):
                block = jnp.where(slots == length + u, rows[u], block)
            dst[b] = block.astype(BF16)

    for cp in loc[3:5]:
        cp.wait()
    for cp in kv_copies:
        cp.wait_recv()
    for cp in q_copies:
        cp.wait_recv()
    acc[...] = jnp.zeros_like(acc)
    per = kall.shape[1] // POS_TILE if kall.shape[1] >= POS_TILE else 1
    tile = kall.shape[1] // per

    def attend(i, carry):
        xi = lax.div(i, per)
        at_row = pl.multiple_of(lax.rem(i, per) * tile, tile)
        keys = kall[xi, pl.ds(at_row, tile), :]
        values = vall[xi, pl.ds(at_row, tile), :]
        queries = qa[...].reshape(ZL * 2 * ROWS, HEAD)
        w = weights_of(dot_t(queries, keys)).astype(BF16)
        wide = jnp.concatenate([values, jnp.ones((tile, HEAD), BF16)], axis=1)
        acc[...] += dot(w, wide)
        return carry

    lax.fori_loop(0, XN * per, attend, 0)

    QR = 2 * ROWS
    eye = lax.broadcasted_iota(jnp.int32, (QR, 128), 0) == lax.broadcasted_iota(jnp.int32, (QR, 128), 1)
    upper = lax.broadcasted_iota(jnp.int32, (16, 128), 0) < 8
    p_copies = []
    for o in range(ZL):
        zo = lax.rem(zl + o, ZL)
        at_row = pl.multiple_of(zo * QR, 8)
        psend[o, pl.ds(0, QR), :] = acc[pl.ds(at_row, QR), pl.ds(0, HEAD)].astype(BF16)
        totals = acc[pl.ds(at_row, QR), pl.ds(HEAD, HEAD)]
        line = jnp.sum(jnp.where(eye, totals, 0.0), axis=0, keepdims=True)
        coarse = line.astype(BF16).astype(F32)
        psend[o, pl.ds(QR, 16), :] = jnp.where(upper, coarse, line - coarse).astype(BF16)
        if o > 0:
            p_copies.append(push(rc(psend.at[o], precv.at[o], ps.at[o], pr.at[o], at(zl_=zo))))
    both = psend[0].astype(F32)
    for o in range(1, ZL):
        p_copies[o - 1].wait_recv()
        both = both + precv[o].astype(F32)
    line = both[QR : QR + 1] + both[QR + 8 : QR + 9]
    column = jnp.sum(jnp.where(eye, line, 0.0), axis=1, keepdims=True)
    attended = ((both[:QR] + suf_w) / (column + suf_t)).astype(BF16)
    heads = jnp.concatenate([attended[:ROWS], attended[ROWS:]], axis=1)

    loc[0].wait()
    ordered = dot(perm[...], heads).astype(BF16)
    GRP = 4 * ZH
    HALF = YN * GRP
    WC = width // 9 if width % 1152 == 0 and width > 1152 else width
    for i in range(width // WC):
        cols = pl.ds(i * WC, WC)
        res = dot(ordered, woutv[:, cols])
        for kk in range(KN):
            br[kk, :, cols] = res[kk * HALF : (kk + 1) * HALF]
    mine = br[k]
    if KN > 1:
        csend[...] = br[1 - k].astype(BF16)
        cp = push(rc(csend, crecv, bcs, bcr, at(k_=1 - k)))
        cp.wait_recv()
        mine = mine + crecv[...].astype(F32)
    for yy in range(YN):
        s1[yy] = mine[yy * GRP : (yy + 1) * GRP]
    hw = width // 2
    by_copies = []
    for o in range(1, YN):
        yo = lax.rem(y + o, YN)
        v = s1[yo]
        ysend[o] = jnp.concatenate([v[:, :hw], v[:, hw:]], axis=0).astype(BF16)
        by_copies.append(push(rc(ysend.at[o], yrecv.at[o], bys.at[o], byr.at[o], at(y_=yo))))
    total = s1[y]
    for o in range(1, YN):
        by_copies[o - 1].wait_recv()
        v = yrecv[o].astype(F32)
        total = total + jnp.concatenate([v[:GRP], v[GRP:]], axis=1)
    branch = total[0:4]
    if ZH > 1:
        qw = width // 4
        first = zh == 0
        other = jnp.where(first, total[4:8], total[0:4])
        zsend[...] = jnp.concatenate(
            [other[:, i * qw : (i + 1) * qw] for i in range(4)], axis=0
        ).astype(BF16)
        cp = push(rc(zsend, zrecv, bzs, bzr, at(zh_=1 - zh)))
        cp.wait_recv()
        v = zrecv[...].astype(F32)
        branch = jnp.where(first, total[0:4], total[4:8]) + jnp.concatenate(
            [v[i * 4 : (i + 1) * 4] for i in range(4)], axis=1
        )
    branch = branch[0:STEPS]
    square = jnp.mean(branch * branch, axis=-1, keepdims=True)
    scaled = branch * lax.rsqrt(square + epsilon) * gain[...].astype(F32)
    out_h[...] = hid[...].astype(F32) + scaled

    for cp in a_copies + sends:
        cp.wait_send()
    for to in range(XN):
        @pl.when(x != to)
        def _():
            w_copy(to).wait_send()


def order_matrix(dims):
    ZH, YN, KN, ZL = dims
    beams = ZH * YN * KN
    m = np.zeros((KN * YN * ZH * 4, STEPS * beams), np.float32)
    for kk in range(KN):
        for yy in range(YN):
            for hh in range(ZH):
                for t in range(STEPS):
                    m[((kk * YN + yy) * ZH + hh) * 4 + t, t * beams + (hh * YN + yy) * KN + kk] = 1.0
    return m


def body(
    dims,
    hidden_in,
    pre_gain,
    post_gain,
    w_query,
    key_projection_weight,
    value_projection_weight,
    w_out,
    prompt_rotated_keys,
    prompt_value_rows,
    suffix_key_cache,
    suffix_value_cache,
    parents,
    lengths,
):
    ZH, YN, KN, ZL = dims
    ZN = ZH * ZL
    YK = YN * KN
    beams = ZH * YK
    rows = STEPS * beams
    width = hidden_in.shape[3]
    slots = suffix_key_cache.shape[2]
    positions = prompt_rotated_keys.shape[0]
    prompt_total = positions * ZL * XN
    depth = width // ZL
    J = -(-depth // 128)
    TJ = -(-(STEPS * J) // 16) * 16
    hid = hidden_in.reshape(STEPS, width)
    rows_float = hid.astype(F32)
    mean_square = jnp.mean(rows_float * rows_float, axis=-1, keepdims=True)
    normed = (rows_float * lax.rsqrt(mean_square + epsilon) * pre_gain.astype(F32)).astype(BF16)
    tiles = jnp.pad(normed.reshape(STEPS, ZL, depth), ((0, 0), (0, 0), (0, J * 128 - depth)))
    tiles = tiles.reshape(STEPS, ZL, J, 128).transpose(1, 0, 2, 3).reshape(ZL, STEPS * J, 128)
    tiles = jnp.pad(tiles, ((0, 0), (0, TJ - STEPS * J), (0, 0)))

    at_context = lax.axis_index("context")
    own = lax.dynamic_slice_in_dim(lengths, at_context // XN * XN, XN)
    place = (prompt_total + own[:, None] + jnp.arange(STEPS, dtype=jnp.int32)[None, :]).reshape(-1, 1)
    frequency = rope_base ** (-2.0 * jnp.arange(HEAD // 2, dtype=F32) / HEAD)
    angles = place.astype(F32) * frequency
    is_value = at_context % XN == 3
    cosine = jnp.where(is_value, 1.0, jnp.cos(angles))
    sine = jnp.where(is_value, 0.0, jnp.sin(angles))
    cos_rows = jnp.concatenate([cosine, cosine], axis=1)
    sin_rows = jnp.concatenate([-sine, sine], axis=1)

    perm = jnp.asarray(order_matrix(dims), BF16)
    hbm = pl.BlockSpec(memory_space=pl.ANY)
    vmem = pl.BlockSpec(memory_space=pltpu.VMEM)
    smem = pl.BlockSpec(memory_space=pltpu.SMEM)
    wrows = w_query.shape[0]
    grp = 4 * ZH
    half = YN * grp
    V = pltpu.VMEM
    D = pltpu.SemaphoreType.DMA
    scratch = [
        V((ZN, TJ, 128), BF16),
        V((ZN * TJ, 128), F32),
        V((XN * YK, STEPS * ZN, J * 128), BF16),
        V((XN, wrows, HEAD), BF16),
        V((J * 128, HEAD), BF16),
        V((YK * STEPS * ZN, HEAD), F32),
        V((XN, ZL, rows, HEAD), BF16),
        V((XN, ZL, rows, HEAD), BF16),
        V((XN, rows, HEAD), BF16),
        V((XN, rows, HEAD), BF16),
        V((ZL, 2, rows, HEAD), BF16),
        V((XN, positions, HEAD), BF16),
        V((XN, positions, HEAD), BF16),
        V((ZL * 2 * rows, 2 * HEAD), F32),
        V((ZL, 2 * rows + 16, HEAD), BF16),
        V((ZL, 2 * rows + 16, HEAD), BF16),
        V(w_out.shape, BF16),
        V((beams, slots, HEAD), BF16),
        V((beams, slots, HEAD), BF16),
        V((rows, 128), jnp.int32),
        V((STEPS, rows, 128), jnp.int32),
        V((rows, HEAD), F32),
        V((KN, half, width), F32),
        V((half, width), BF16),
        V((half, width), BF16),
        V((YN, grp, width), F32),
        V((YN, 2 * grp, width // 2), BF16),
        V((YN, 2 * grp, width // 2), BF16),
        V((16, width // 4), BF16),
        V((16, width // 4), BF16),
        D((ZN,)), D((ZN,)), D((XN,)), D((XN,)), D((2, XN)), D((2, XN)), D((XN,)), D((XN,)),
        D((XN, YN)), D((XN, YN)), D((XN, YN)), D((XN, YN)), D((XN, ZL)), D((XN, ZL)),
        D((XN,)), D((XN,)), D((ZL,)), D((ZL,)), D((ZL,)), D((ZL,)),
        D, D, D((YN,)), D((YN,)), D, D, D((8,)),
    ]
    hidden_out, keys_out, values_out = pl.pallas_call(
        functools.partial(kernel, dims, prompt_total),
        out_shape=(
            jax.ShapeDtypeStruct((STEPS, width), F32),
            jax.ShapeDtypeStruct((beams, slots, HEAD), BF16),
            jax.ShapeDtypeStruct((beams, slots, HEAD), BF16),
        ),
        in_specs=[vmem] * 6 + [hbm] * 8 + [smem] * 2,
        out_specs=(vmem, vmem, vmem),
        scratch_shapes=scratch,
        compiler_params=pltpu.CompilerParams(
            collective_id=0, has_side_effects=True, vmem_limit_bytes=48 * 1024 * 1024
        ),
    )(
        tiles,
        hid,
        post_gain.reshape(1, width),
        cos_rows,
        sin_rows,
        perm,
        w_query,
        key_projection_weight,
        value_projection_weight,
        w_out,
        prompt_rotated_keys,
        prompt_value_rows,
        suffix_key_cache.reshape(beams, slots, HEAD),
        suffix_value_cache.reshape(beams, slots, HEAD),
        parents.reshape(STEPS, beams),
        lengths,
    )
    return (
        hidden_out.reshape(STEPS, 1, 1, width),
        keys_out.reshape(1, beams, slots, HEAD),
        values_out.reshape(1, beams, slots, HEAD),
    )


def solution(mesh, dims=(2, 4, 2, 8)):
    placed = (
        P(None, "context", "sample", None),
        P(),
        P(),
        P("context", "sample"),
        P("context", "sample"),
        P("context", "sample"),
        P("sample", None),
        P("context", "sample"),
        P("context", "sample"),
        P("context", None, None, "sample"),
        P("context", None, None, "sample"),
        P(None, "context", None),
        P(),
    )
    return jax.shard_map(
        functools.partial(body, dims),
        mesh=mesh,
        in_specs=placed,
        out_specs=(
            P(None, "context", "sample", None),
            P("context", None, None, "sample"),
            P("context", None, None, "sample"),
        ),
        check_vma=False,
    )
```

time: 2000 us -> 117 us (0.06)
  waiting for transfers between devices: 1330 us -> 0 us
  blocking collectives: 330 us -> 0 us
  other arithmetic: 138 us -> 2.02 us
  Pallas kernels: 0 us -> 97.1 us
  local copies, waits for them, and re-layouts: 84.7 us -> 15.6 us
  starting transfers between devices: 57.5 us -> 0 us
  matrix products: 28.5 us -> 0 us
    reduce_scatter x3 -> x0, waiting for transfers between devices: 474 us -> none  [body(): lax.psum_scatter(weighted, 'context', scatter_dimension=0, tiled=True)]
    psum x1 -> x0, waiting for transfers between devices: 450 us -> none  [body(): summed = lax.psum(partial_sums, 'context')]
    unnamed x6 -> x0, waiting for transfers between devices: 275 us -> none
    unnamed x1 -> x0, blocking collectives: 208 us -> none
    all_to_all x3 -> x0, waiting for transfers between devices: 133 us -> none  [body(): lax.all_to_all(normed, 'context', split_axis=2, concat_axis=0, tiled=True)]
    all_gather x3 -> x0, blocking collectives: 122 us -> none  [body(): lax.all_gather(spread, 'sample', axis=1, tiled=True)]
    all_to_all x3 -> x0, other arithmetic: 106 us -> none  [body(): lax.all_to_all(normed, 'context', split_axis=2, concat_axis=0, tiled=True)]
    pallas_call x0 -> x1, Pallas kernels: none -> 97.1 us  [body(): pl.pallas_call(functools.partial(kernel, dims, prompt_total), out_shape=(...]
  transfers between devices with their start and end apart: 8 -> 0, of which waited for: 8 -> 0; matrix products, arithmetic and copies ran while one was open for 7% -> 0% of each run, Pallas kernels for 0% -> 0%
where the time goes in v1:
time: 117 us; the launch traced here: 115 us
  Pallas kernels  97.1 us (83%)
  local copies, waits for them, and re-layouts  15.6 us (13%)
  other arithmetic  2.02 us (2%)
    pallas_call x1, Pallas kernels, body(): pl.pallas_call(functools.partial(kernel, dims, prompt_total), out_shape=(...  97.1 us
    unnamed x26, local copies, waits for them, and re-layouts  13.2 us

profile of v1, /device:TPU:1, one launch (start us, length us, event | category | flops | bytes accessed | tf_op | source)
XLA Modules:
  0.0 115.5 jit_solution(6073646984304743121)
XLA Ops:
  0.7 0.7 dynamic-slice_add_fusion
  1.4 0.9 multiply_reduce_fusion
  2.4 0.1 convert_element_type.34
  2.5 0.7 copy.23
  3.2 0.7 reshape.87.gain
  3.9 0.8 reshape.95
  4.7 0.1 fusion.2
  4.9 0.9 reshape.94
  5.7 0.1 multiply_convert_fusion
  5.9 1.7 %copy-done = bf16[256,4608]{1,0:T(8,128)(2,1)S(1)} copy-done((bf16[256,4608]{1,0:T(8,128)(2,1)S(1)}, bf16[256,4608]{1,0:T(8,128)(2,1)}, u32[]{:S(2)}) %copy-start) | copy-done | bytes 2359320
  7.5 1.0 copy-done.1
  8.6 1.0 copy-done.2
  9.6 0.8 copy-done.3
  10.4 0.9 copy-done.4
  11.3 0.9 copy-done.5
  12.3 0.9 copy-done.6
  13.2 0.8 copy-done.7
  13.9 0.8 copy-done.8
  14.7 0.7 copy-done.9
  15.4 0.7 copy-done.10
  16.1 97.1 %shard_map.157 = (f32[3,4608]{1,0:T(4,128)S(1)}, bf16[16,128,128]{2,1,0:T(8,128)(2,1)S(1)}, bf16[16,128,128]{2,1,0:T(8,128)(2,1)S(1)}) custom-call(bf16[8,16,128]{2,1,0:T(8,128)(2,1)S(1)} %pad.9.tiles, bf16[3,4608]{1,0:T(4,128)(2,1)S(1)} %bitcast.21, bf16[1,4608]{1,0:T(2,128)(2,1)S(1)} %reshape.87.gain, f32[12,128]{1,0:T(8,128)S(1)} %get-tuple-element.18.cos_rows, ...), custom_call_target="tpu_custom_call" | custom-call | tf_op jit(solution)/shard_map/pallas_call | solution.py:514
  113.2 0.7 copy.20
  113.9 0.8 copy.26
  114.7 0.8 copy.27
  (18 shorter events, 0.2 us)
Async XLA Ops:
  5.9 1.7 %copy-start = (bf16[256,4608]{1,0:T(8,128)(2,1)S(1)}, bf16[256,4608]{1,0:T(8,128)(2,1)}, u32[]{:S(2)}) copy-start(bf16[256,4608]{1,0:T(8,128)(2,1)} %wout.1) | copy-start | bytes 7077892
  7.5 1.0 copy-start.1
  8.6 1.0 copy-start.2
  9.6 0.8 copy-start.3
  10.4 0.9 copy-start.4
  11.3 0.9 copy-start.5
  12.3 0.9 copy-start.6
  13.2 0.8 copy-start.7
  13.9 0.8 copy-start.8
  14.7 0.7 copy-start.9
  15.4 0.7 copy-start.10

commit v2 on v1

--- a/solution.py
+++ b/solution.py
@@ -17,6 +17,10 @@
 query_scale = 144.0 ** (-0.5)
 rope_base = 10000.0
 logit_cap = 50.0
+TURN = 2 * np.pi
+TURN_A = 6.28125
+TURN_B = float(np.float32(np.round((TURN - TURN_A) * 2.0**20) / 2.0**20))
+TURN_C = float(TURN - TURN_A - TURN_B)
 MESH = pl.DeviceIdType.MESH
 F32 = jnp.float32
 BF16 = jnp.bfloat16
@@ -36,9 +40,9 @@
 
 def kernel(
     dims, prompt_total,
-    tiles, hid, gain, cos_rows, sin_rows, perm, wq, wk, wv, wout, pk, pv, kc, vc, par, lens,
+    hid, pre_gain, post_gain, freq, perm, wq, wk, wv, wout, pk, pv, kc, vc, par, lens,
     out_h, out_k, out_v,
-    a1, a1f, xb, wf, wp, yf, sred, rred, g, gf, qa, kall, vall, acc, psend, precv,
+    tiles, tilesf, cos_rows, sin_rows, a1, a1f, xb, wf, wp, yf, sred, rred, g, gf, qa, kall, vall, acc, psend, precv,
     woutv, kcv, vcv, ancv, freshv, freshk, br, csend, crecv, s1, ysend, yrecv, zsend, zrecv,
     as_, ar, ws, wr, ks, kr, xs, xr, ys, yr, cs, cr, rs, rr, gs, gr, qs, qr, ps, pr,
     bcs, bcr, bys, byr, bzs, bzr, ls,
@@ -84,6 +88,33 @@
     barrier = pltpu.get_barrier_semaphore()
     for peer in peers:
         pl.semaphore_signal(barrier, inc=1, device_id=peer, device_id_type=MESH)
+
+    part_width = width // ZL
+    J = xb.shape[2] // 128
+    TJ = a1.shape[1]
+    hid_f = hid[...].astype(F32)
+    gain_row = pre_gain[...].reshape(1, width).astype(F32)
+    pieces = []
+    for t in range(STEPS):
+        row = hid_f[t : t + 1]
+        mean_square = jnp.mean(row * row, axis=-1, keepdims=True)
+        pieces.append(row * lax.rsqrt(mean_square + epsilon) * gain_row)
+    rows3 = jnp.concatenate(pieces, axis=0)
+    lane1 = lax.broadcasted_iota(jnp.int32, (STEPS, 128), 1)
+    tilesf[...] = jnp.zeros_like(tilesf)
+    for part in range(ZL):
+        for j in range(J):
+            start = part * part_width + j * 128
+            got = min(128, (part + 1) * part_width - start)
+            base = min(start, width - 128)
+            shift = start - base
+            seg = rows3[:, base : base + 128]
+            if shift:
+                seg = pltpu.roll(seg, 128 - shift, 1)
+            if got < 128:
+                seg = jnp.where(lane1 < got, seg, 0.0)
+            tilesf[part, pl.ds(j * STEPS, STEPS), :] = seg
+    tiles[...] = tilesf[...].astype(BF16)
     pl.semaphore_wait(barrier, len(peers))
 
     a_copies = []
@@ -125,15 +156,13 @@
     for cp in a_copies:
         cp.wait_recv()
 
-    TJ = a1.shape[1]
-    J = xb.shape[2] // 128
     for i in range(ZN):
         a1f[pl.ds(i * TJ, TJ), :] = a1[i].astype(F32)
     b_own = (x * YN + y) * KN + k
     for t in range(STEPS):
         for j in range(J):
             xb[b_own, pl.ds(t * ZN, ZN), pl.ds(j * 128, 128)] = a1f[
-                pl.ds(t * J + j, ZN, stride=TJ), :
+                pl.ds(j * STEPS + t, ZN, stride=TJ), :
             ].astype(BF16)
 
     def blk(x_, y_, k_):
@@ -223,6 +252,20 @@
                     rc(sred.at[ox, o], rred.at[ox, o], rs.at[ox, o], rr.at[ox, o], at(zl_=zo))
                 )
 
+    at_row = lax.broadcasted_iota(jnp.int32, (16, 128), 0)
+    place = jnp.zeros((16, 128), jnp.int32)
+    for i in range(XN):
+        for t in range(STEPS):
+            place = jnp.where(at_row == i * STEPS + t, lens[zl * XN + i] + (prompt_total + t), place)
+    angles = place.astype(F32) * freq[...]
+    turns = jnp.round(angles * (1.0 / TURN))
+    angles = ((angles - turns * TURN_A) - turns * TURN_B) - turns * TURN_C
+    lower = lax.broadcasted_iota(jnp.int32, (16, 128), 1) < HEAD // 2
+    sines = jnp.sin(angles)
+    plain = x == 3
+    cos_rows[...] = jnp.where(plain, 1.0, jnp.cos(angles))
+    sin_rows[...] = jnp.where(plain, 0.0, jnp.where(lower, -sines, sines))
+
     scale = jnp.where(x < 2, query_scale, 1.0).astype(F32)
     g_copies = {}
     for ox in (0,) + X_ORDER:
@@ -254,12 +297,12 @@
     length = lens[c]
     for cp in loc[1:3]:
         cp.wait()
-    p0 = [par[0, b] for b in range(BEAMS)]
-    p1 = [par[1, b] for b in range(BEAMS)]
-    p2 = [par[2, b] for b in range(BEAMS)]
-    first_of = [par[0, p1[b]] for b in range(BEAMS)]
-    mid_of = [par[1, p2[b]] for b in range(BEAMS)]
-    last_of = [par[0, mid_of[b]] for b in range(BEAMS)]
+    p0 = [par[0, 0, b] for b in range(BEAMS)]
+    p1 = [par[1, 0, b] for b in range(BEAMS)]
+    p2 = [par[2, 0, b] for b in range(BEAMS)]
+    first_of = [par[0, 0, p1[b]] for b in range(BEAMS)]
+    mid_of = [par[1, 0, p2[b]] for b in range(BEAMS)]
+    last_of = [par[0, 0, mid_of[b]] for b in range(BEAMS)]
     never = jnp.int32(-1)
     for b in range(BEAMS):
         own = jnp.int32(b)
@@ -396,8 +439,9 @@
         )
     branch = branch[0:STEPS]
     square = jnp.mean(branch * branch, axis=-1, keepdims=True)
-    scaled = branch * lax.rsqrt(square + epsilon) * gain[...].astype(F32)
-    out_h[...] = hid[...].astype(F32) + scaled
+    scaled = branch * lax.rsqrt(square + epsilon) * post_gain[...].reshape(1, width).astype(F32)
+    for t in range(STEPS):
+        out_h[t, 0] = hid[t : t + 1].astype(F32) + scaled[t : t + 1]
 
     for cp in a_copies + sends:
         cp.wait_send()
@@ -447,27 +491,11 @@
     depth = width // ZL
     J = -(-depth // 128)
     TJ = -(-(STEPS * J) // 16) * 16
-    hid = hidden_in.reshape(STEPS, width)
-    rows_float = hid.astype(F32)
-    mean_square = jnp.mean(rows_float * rows_float, axis=-1, keepdims=True)
-    normed = (rows_float * lax.rsqrt(mean_square + epsilon) * pre_gain.astype(F32)).astype(BF16)
-    tiles = jnp.pad(normed.reshape(STEPS, ZL, depth), ((0, 0), (0, 0), (0, J * 128 - depth)))
-    tiles = tiles.reshape(STEPS, ZL, J, 128).transpose(1, 0, 2, 3).reshape(ZL, STEPS * J, 128)
-    tiles = jnp.pad(tiles, ((0, 0), (0, TJ - STEPS * J), (0, 0)))
-
-    at_context = lax.axis_index("context")
-    own = lax.dynamic_slice_in_dim(lengths, at_context // XN * XN, XN)
-    place = (prompt_total + own[:, None] + jnp.arange(STEPS, dtype=jnp.int32)[None, :]).reshape(-1, 1)
-    frequency = rope_base ** (-2.0 * jnp.arange(HEAD // 2, dtype=F32) / HEAD)
-    angles = place.astype(F32) * frequency
-    is_value = at_context % XN == 3
-    cosine = jnp.where(is_value, 1.0, jnp.cos(angles))
-    sine = jnp.where(is_value, 0.0, jnp.sin(angles))
-    cos_rows = jnp.concatenate([cosine, cosine], axis=1)
-    sin_rows = jnp.concatenate([-sine, sine], axis=1)
+    frequency = 1.0 / rope_base ** (np.arange(HEAD // 2) * 2.0 / HEAD)
+    freq = jnp.asarray(np.concatenate([frequency, frequency])[None], F32)
 
     perm = jnp.asarray(order_matrix(dims), BF16)
-    hbm = pl.BlockSpec(memory_space=pl.ANY)
+    hbm = pl.BlockSpec(memory_space=pltpu.HBM)
     vmem = pl.BlockSpec(memory_space=pltpu.VMEM)
     smem = pl.BlockSpec(memory_space=pltpu.SMEM)
     wrows = w_query.shape[0]
@@ -476,6 +504,10 @@
     V = pltpu.VMEM
     D = pltpu.SemaphoreType.DMA
     scratch = [
+        V((ZL, TJ, 128), BF16),
+        V((ZL, TJ, 128), F32),
+        V((16, 128), F32),
+        V((16, 128), F32),
         V((ZN, TJ, 128), BF16),
         V((ZN * TJ, 128), F32),
         V((XN * YK, STEPS * ZN, J * 128), BF16),
@@ -514,22 +546,21 @@
     hidden_out, keys_out, values_out = pl.pallas_call(
         functools.partial(kernel, dims, prompt_total),
         out_shape=(
-            jax.ShapeDtypeStruct((STEPS, width), F32),
+            jax.ShapeDtypeStruct((STEPS, 1, 1, width), F32),
             jax.ShapeDtypeStruct((beams, slots, HEAD), BF16),
             jax.ShapeDtypeStruct((beams, slots, HEAD), BF16),
         ),
-        in_specs=[vmem] * 6 + [hbm] * 8 + [smem] * 2,
+        in_specs=[vmem] * 5 + [hbm] * 8 + [smem] * 2,
         out_specs=(vmem, vmem, vmem),
         scratch_shapes=scratch,
         compiler_params=pltpu.CompilerParams(
-            collective_id=0, has_side_effects=True, vmem_limit_bytes=48 * 1024 * 1024
+            collective_id=0, has_side_effects=True, vmem_limit_bytes=63 * 1024 * 1024
         ),
     )(
-        tiles,
-        hid,
-        post_gain.reshape(1, width),
-        cos_rows,
-        sin_rows,
+        hidden_in.reshape(STEPS, width),
+        pre_gain,
+        post_gain,
+        freq,
         perm,
         w_query,
         key_projection_weight,
@@ -539,11 +570,11 @@
         prompt_value_rows,
         suffix_key_cache.reshape(beams, slots, HEAD),
         suffix_value_cache.reshape(beams, slots, HEAD),
-        parents.reshape(STEPS, beams),
+        parents,
         lengths,
     )
     return (
-        hidden_out.reshape(STEPS, 1, 1, width),
+        hidden_out,
         keys_out.reshape(1, beams, slots, HEAD),
         values_out.reshape(1, beams, slots, HEAD),
     )

time: 117 us -> 105 us (0.90)
  local copies, waits for them, and re-layouts: 15.6 us -> 5.21 us
  other arithmetic: 2.02 us -> 0 us
    unnamed x26 -> x3, local copies, waits for them, and re-layouts: 13.2 us -> 5.21 us
where the time goes in v2:
time: 105 us; the launch traced here: 104 us
  Pallas kernels  98 us (93%)
  local copies, waits for them, and re-layouts  5.21 us (5%)
    pallas_call x1, Pallas kernels, body(): pl.pallas_call(functools.partial(kernel, dims, prompt_total), out_shape=(...  98 us
    unnamed x3, local copies, waits for them, and re-layouts  5.21 us

profile of v2, /device:TPU:1, one launch (start us, length us, event | category | flops | bytes accessed | tf_op | source)
XLA Modules:
  0.0 103.8 jit_solution(11484925689890907268)
XLA Ops:
  0.6 98.0 %shard_map.166 = (f32[3,1,1,4608]{3,2,1,0:T(1,128)}, bf16[16,128,128]{2,1,0:T(8,128)(2,1)}, bf16[16,128,128]{2,1,0:T(8,128)(2,1)}) custom-call(bf16[3,4608]{1,0:T(4,128)(2,1)} %bitcast.9, bf16[4608]{0:T(1024)(128)(2,1)} %pre_gain.1, bf16[4608]{0:T(1024)(128)(2,1)} %post_gain.1, f32[1,128]{1,0:T(1,128)} %constant.4.clone.freq, ...), custom_call_target="tpu_custom_call" | custom-call | tf_op jit(solution)/shard_map/pallas_call | solution.py:546
  98.6 1.4 %copy.21 = f32[3,1,1,4608]{3,2,1,0:T(1,128)} copy(f32[3,1,1,4608]{3,2,1,0:T(1,128)} %get-tuple-element.12) | data formatting | bytes 110592
  100.1 1.9 %copy.22 = bf16[1,16,128,128]{3,2,1,0:T(8,128)(2,1)} copy(bf16[1,16,128,128]{3,2,1,0:T(8,128)(2,1)} %bitcast.6) | data formatting | bytes 1048576
  102.0 1.9 %copy.23 = bf16[1,16,128,128]{3,2,1,0:T(8,128)(2,1)} copy(bf16[1,16,128,128]{3,2,1,0:T(8,128)(2,1)} %bitcast.5) | data formatting | bytes 1048576

commit v3 on v2

v3 whole, which is shorter than its diff:
```python
import functools

import jax
import jax.numpy as jnp
import numpy as np
from jax import lax
from jax.experimental import pallas as pl
from jax.experimental.pallas import tpu as pltpu
from jax.sharding import PartitionSpec as P

HEAD = 128
STEPS = 3
XN = 4
BLOCK = 16
CHUNKS = 3
POS_TILE = 512

epsilon = 1e-06
query_scale = 144.0 ** (-0.5)
rope_base = 10000.0
logit_cap = 50.0
TURN = 2 * np.pi
TURN_A = 6.28125
TURN_B = float(np.float32(np.round((TURN - TURN_A) * 2.0**20) / 2.0**20))
TURN_C = float(TURN - TURN_A - TURN_B)
MESH = pl.DeviceIdType.MESH
F32 = jnp.float32
BF16 = jnp.bfloat16
AROUND = (1, 3, 2)


def weights_of(scores):
    return jnp.exp(logit_cap * jnp.tanh(scores * (1.0 / logit_cap)))


def dot_t(a, b):
    return lax.dot_general(a, b, (((1,), (1,)), ((), ())), preferred_element_type=F32)


def dot(a, b):
    return jnp.dot(a, b, preferred_element_type=F32)


def iota(shape, axis):
    return lax.broadcasted_iota(jnp.int32, shape, axis)


def kernel(
    dims, prompt_total,
    hid, pre_gain, post_gain, freq, perm, wq, wk, wv, wout, pk, pv, kc, vc, par, lens,
    out_h, out_f,
    tiles, tilesf, cos_rows, sin_rows, a1, a1f, xb, wz, yf, sred, rred, g, gf, qa, kall, vall, acc,
    psend, precv, both, osend, orecv, woutv, kcv, vcv, ancv, freshv, br, csend, crecv, s1, ysend,
    yrecv, zsend, zrecv,
    as_, ar, ws, wr, wzs, wzr, ks, kr, pxs, pxr, pys, pyr, rys, ryr, rxs, rxr, cs, cr, rs, rr, gs,
    gr, qs, qr, ps, pr, os_, or_, bcs, bcr, bys, byr, bzs, bzr, ls,
):
    ZH, YN, KN, ZL = dims
    ZN = ZH * ZL
    PN = ZL // 2
    GN = 2 * ZH
    YK = YN * KN
    BEAMS = ZH * YK
    ROWS = STEPS * BEAMS
    s = lax.axis_index("sample")
    c = lax.axis_index("context")
    zh = lax.div(s, YK)
    y = lax.div(lax.rem(s, YK), KN)
    k = lax.rem(s, KN)
    zl = lax.div(c, XN)
    x = lax.rem(c, XN)
    z = zh * ZL + zl
    q = lax.div(zl, PN)
    p = lax.rem(zl, PN)
    width = hid.shape[1]

    def at(zh_=None, y_=None, k_=None, zl_=None, x_=None):
        zh_ = zh if zh_ is None else zh_
        y_ = y if y_ is None else y_
        k_ = k if k_ is None else k_
        zl_ = zl if zl_ is None else zl_
        x_ = x if x_ is None else x_
        return {"sample": zh_ * YK + y_ * KN + k_, "context": zl_ * XN + x_}

    def rc(src, dst, ssem, rsem, where):
        return pltpu.make_async_remote_copy(
            src_ref=src, dst_ref=dst, send_sem=ssem, recv_sem=rsem,
            device_id=where, device_id_type=MESH,
        )

    sends = []

    def push(cp):
        cp.start()
        sends.append(cp)
        return cp

    def x_of(o):
        return lax.rem(x + o + XN, XN)

    def y_of(o):
        return lax.rem(y + o + YN, YN)

    def p_of(o):
        return lax.rem(p + o + PN, PN)

    def half_at(m):
        zz = lax.rem(z + PN * m, ZN)
        zl_ = lax.rem(zz, ZL)
        return at(zh_=lax.div(zz, ZL), zl_=zl_), lax.div(zl_, PN)

    across = at(zl_=(1 - q) * PN + p)

    peers = [half_at(m)[0] for m in range(1, GN)]
    peers += [at(zl_=q * PN + p_of(o)) for o in range(1, PN)]
    peers += [at(x_=x_of(o)) for o in range(1, XN)]
    peers += [at(y_=y_of(o)) for o in range(1, YN)]
    if KN > 1:
        peers += [at(k_=1 - k)]
    if ZH == 1:
        assert GN == 2
    barrier = pltpu.get_barrier_semaphore()
    for peer in peers:
        pl.semaphore_signal(barrier, inc=1, device_id=peer, device_id_type=MESH)

    loc = [
        pltpu.make_async_copy(wout, woutv, ls.at[1]),
        pltpu.make_async_copy(kc, kcv, ls.at[2]),
        pltpu.make_async_copy(vc, vcv, ls.at[3]),
        pltpu.make_async_copy(pk, kall.at[x], ls.at[4]),
        pltpu.make_async_copy(pv, vall.at[x], ls.at[5]),
    ]
    for cp in loc:
        cp.start()

    J = width // 256
    TJ = a1.shape[1]
    hid_f = hid[...].astype(F32)
    mean_square = jnp.mean(hid_f * hid_f, axis=-1, keepdims=True)
    normed = hid_f * lax.rsqrt(mean_square + epsilon) * pre_gain[...].reshape(1, width).astype(F32)
    for part in range(2):
        for j in range(J):
            start = (part * J + j) * 128
            tilesf[part, pl.ds(j * STEPS, STEPS), :] = normed[:, start : start + 128]
        if TJ > J * STEPS:
            tilesf[part, pl.ds(J * STEPS, TJ - J * STEPS), :] = jnp.zeros((TJ - J * STEPS, 128), F32)
    tiles[...] = tilesf[...].astype(BF16)
    pl.semaphore_wait(barrier, len(peers))

    mine = lax.div(z, PN)
    a_copies = []
    for m in (2, 1, 3):
        if m < GN:
            where, q_to = half_at(m)
            a_copies.append(push(rc(tiles.at[q_to], a1.at[mine], as_.at[m], ar.at[m], where)))

    half = wq.shape[1] // 2
    w_src = [wq.at[:, pl.ds(0, half)], wq.at[:, pl.ds(half, half)], wk, wv]

    def w_copy(to):
        return rc(w_src[to], wz.at[p, x], ws.at[to], wr.at[x], at(x_=to))

    def w_local(to):
        return pltpu.make_async_copy(w_src[to], wz.at[p, x], ls.at[0])

    for to in range(XN):
        @pl.when(x != to)
        def _():
            w_copy(to).start()

        @pl.when(x == to)
        def _():
            w_local(to).start()

    kv_copies = []

    def send_prompt(which, o):
        src, dst = ((pk, kall), (pv, vall))[which]
        kv_copies.append(push(rc(src, dst.at[x], ks.at[which, o], kr.at[which, o], at(x_=x_of(o)))))

    a1[mine] = tiles[q]
    for to in range(XN):
        @pl.when(x != to)
        def _():
            rc(w_src[to], wz.at[p, to], ws.at[to], wr.at[to], at(x_=to)).wait_recv()

        @pl.when(x == to)
        def _():
            w_local(to).wait()
    wz_copies = []
    for o in range(1, PN):
        wz_copies.append(
            push(rc(wz.at[p], wz.at[p], wzs.at[o], wzr.at[o], at(zl_=q * PN + p_of(o))))
        )
    send_prompt(0, 1)
    send_prompt(0, 3)
    for cp in a_copies:
        cp.wait_recv()

    for i in range(GN):
        a1f[pl.ds(i * TJ, TJ), :] = a1[i].astype(F32)
    own = (x * YN + y) * KN + k
    rest = jnp.zeros((BLOCK - STEPS * GN, 128), F32)
    for j in range(J):
        lines = [a1f[pl.ds(j * STEPS + t, GN, stride=TJ), :] for t in range(STEPS)]
        xb[own, :, pl.ds(j * 128, 128)] = jnp.concatenate(lines + [rest], axis=0).astype(BF16)

    cols = xb.shape[2] // 2

    def blk(ox, oy):
        return (x_of(-ox) * YN + y_of(-oy)) * KN + k

    def first(b):
        return xb.at[b, :, pl.ds(0, cols)]

    def second(b):
        return xb.at[b, :, pl.ds(cols, cols)]

    px, py, ry, rx, cc = {}, {}, {}, {}, {}

    def forward_y(ox):
        b = blk(ox, 0)
        for o in AROUND[: YN - 1]:
            py[ox, o] = push(rc(first(b), first(b), pys.at[ox, o], pyr.at[ox, o], at(y_=y_of(o))))

    def forward_x(oy):
        b = blk(0, oy)
        for o in AROUND:
            rx[oy, o] = push(rc(second(b), second(b), rxs.at[oy, o], rxr.at[oy, o], at(x_=x_of(o))))

    def to_core(ox, oy):
        if KN > 1:
            b = xb.at[blk(ox, oy)]
            cc[ox, oy] = push(rc(b, b, cs.at[ox, oy], cr.at[ox, oy], at(k_=1 - k)))

    y_around = [o for o in AROUND if o < YN]
    for o in AROUND:
        b = blk(0, 0)
        px[o] = push(rc(first(b), first(b), pxs.at[o], pxr.at[o], at(x_=x_of(o))))
        if o < YN:
            ry[o] = push(rc(second(b), second(b), rys.at[o], ryr.at[o], at(y_=y_of(o))))
    if YN > 1:
        for o in y_around:
            b = blk(0, 0)
            py[0, o] = push(rc(first(b), first(b), pys.at[0, o], pyr.at[0, o], at(y_=y_of(o))))
    forward_x(0)
    to_core(0, 0)
    for o in AROUND:
        px[o].wait_recv()
        for o2 in y_around:
            b = blk(o, 0)
            py[o, o2] = push(rc(first(b), first(b), pys.at[o, o2], pyr.at[o, o2], at(y_=y_of(o2))))
        if o < YN:
            ry[o].wait_recv()
            forward_x(o)

    def gather(ox):
        for oy in [0] + y_around:
            if oy > 0:
                py[ox, oy].wait_recv()
            if ox > 0:
                rx[oy, ox].wait_recv()
            if ox > 0 or oy > 0:
                to_core(ox, oy)

    r_copies = {}

    def project(ox):
        for oy in [0] + y_around:
            if KN > 1:
                cc[ox, oy].wait_recv()
        rows = xb[pl.ds(x_of(-ox) * YK, YK)].reshape(YK * BLOCK, xb.shape[2])
        yf[...] = dot(rows, wz[...].reshape(xb.shape[2], HEAD))
        for h in range(2):
            for t in range(STEPS):
                piece = [
                    yf[pl.ds(t * GN + i * 2 + h, YK, stride=BLOCK), :] for i in range(ZH)
                ]
                sred[ox, h, pl.ds(t * BEAMS, BEAMS), :] = jnp.concatenate(piece, axis=0).astype(BF16)
        r_copies[ox] = push(rc(sred.at[ox], rred.at[ox], rs.at[ox], rr.at[ox], across))

    gather(0)
    for cp in wz_copies:
        cp.wait_recv()
    project(0)
    gather(1)
    gather(3)
    project(1)
    gather(2)
    project(3)
    project(2)
    for which, o in ((0, 2), (1, 1), (1, 3), (1, 2)):
        send_prompt(which, o)

    NT = 2 * XN * STEPS
    at_row = iota((NT, 128), 0)
    place = jnp.zeros((NT, 128), jnp.int32)
    for h in range(2):
        for i in range(XN):
            for t in range(STEPS):
                here = lens[(h * PN + p) * XN + i] + (prompt_total + t)
                place = jnp.where(at_row == (h * XN + i) * STEPS + t, here, place)
    angles = place.astype(F32) * freq[...]
    turns = jnp.round(angles * (1.0 / TURN))
    angles = ((angles - turns * TURN_A) - turns * TURN_B) - turns * TURN_C
    lower = iota((NT, 128), 1) < HEAD // 2
    sines = jnp.sin(angles)
    plain = x == 3
    cos_rows[...] = jnp.where(plain, 1.0, jnp.cos(angles))
    sin_rows[...] = jnp.where(plain, 0.0, jnp.where(lower, -sines, sines))

    scale = jnp.where(x < 2, query_scale, 1.0).astype(F32)
    g_copies = {}
    for ox in (0,) + AROUND:
        xo = x_of(-ox)
        r_copies[ox].wait_recv()
        for h in range(2):
            total = sred[ox, h].astype(F32) + rred[ox, h].astype(F32)
            for t in range(STEPS):
                part = total[t * BEAMS : (t + 1) * BEAMS]
                row = pl.ds((h * XN + xo) * STEPS + t, 1)
                turned = part * cos_rows[row, :] + pltpu.roll(part, HEAD // 2, 1) * sin_rows[row, :]
                gf[ox, h, pl.ds(t * BEAMS, BEAMS), :] = (turned * scale).astype(BF16)
        if ox == 0:
            for h in range(2):
                g[h, x] = gf[0, h]
        else:
            g_copies[ox] = push(rc(gf.at[ox], g.at[:, x], gs.at[ox], gr.at[ox], at(x_=xo)))
    for ox in AROUND:
        g_copies[ox].wait_recv()

    q_copies = {}
    for o in range(1, PN):
        q_copies[o] = push(
            rc(g.at[:, pl.ds(0, 2)], qa.at[p], qs.at[o], qr.at[o], at(zl_=q * PN + p_of(o)))
        )
    for h in range(2):
        qa[p, h] = g[h, 0:2]

    for cp in loc[3:5]:
        cp.wait()
    for cp in kv_copies:
        cp.wait_recv()
    per = kall.shape[1] // POS_TILE if kall.shape[1] >= POS_TILE else 1
    tile = kall.shape[1] // per
    QR = 2 * ROWS
    eye = iota((QR, 128), 0) == iota((QR, 128), 1)
    upper = iota((16, 128), 0) < 8

    def with_totals(line):
        coarse = line.astype(BF16).astype(F32)
        return jnp.where(upper, coarse, line - coarse).astype(BF16)

    p_copies = {}
    for o in [0] + [o for o in AROUND if o < PN]:
        if o > 0:
            q_copies[o].wait_recv()
        there = p_of(-o)
        acc[...] = jnp.zeros_like(acc)

        def attend(i, carry):
            xi = lax.div(i, per)
            at_pos = pl.multiple_of(lax.rem(i, per) * tile, tile)
            keys = kall[xi, pl.ds(at_pos, tile), :]
            values = vall[xi, pl.ds(at_pos, tile), :]
            w = weights_of(dot_t(qa[there].reshape(2 * QR, HEAD), keys)).astype(BF16)
            acc[...] += dot(w, jnp.concatenate([values, jnp.ones((tile, HEAD), BF16)], axis=1))
            return carry

        lax.fori_loop(0, XN * per, attend, 0)
        for h in range(2):
            psend[o, h, pl.ds(0, QR), :] = acc[pl.ds(h * QR, QR), pl.ds(0, HEAD)].astype(BF16)
            totals = acc[pl.ds(h * QR, QR), pl.ds(HEAD, HEAD)]
            line = jnp.sum(jnp.where(eye, totals, 0.0), axis=0, keepdims=True)
            psend[o, h, pl.ds(QR, 16), :] = with_totals(line)
        if o > 0:
            p_copies[o] = push(
                rc(psend.at[o], precv.at[o], ps.at[o], pr.at[o], at(zl_=q * PN + there))
            )

    length = lens[c]
    for cp in loc[1:3]:
        cp.wait()
    never = jnp.int32(-1)
    for b in range(BEAMS):
        one = par[1, 0, b]
        two = par[2, 0, b]
        mid = par[1, 0, two]
        me = jnp.int32(b)
        chains = (
            (par[0, 0, b], me, never, never),
            (par[0, 0, one], one, me + BEAMS, never),
            (par[0, 0, mid], mid, two + BEAMS, me + 2 * BEAMS),
        )
        for t in range(STEPS):
            row = t * BEAMS + b
            ancv[pl.ds(row, 1), :] = jnp.full((1, 128), chains[t][0], jnp.int32)
            for u in range(STEPS):
                freshv[u, pl.ds(row, 1), :] = jnp.full((1, 128), chains[t][1 + u], jnp.int32)
    my_q = g[q, 0:2].reshape(QR, HEAD)
    SLOTS = kcv.shape[1]
    anc = ancv[:, :SLOTS]
    anc2 = jnp.concatenate([anc, anc], axis=0)
    in_use = iota((QR, SLOTS), 1) < length
    lane = iota((ROWS, ROWS), 1)
    seen = (lane == freshv[0, :, :ROWS]) | (lane == freshv[1, :, :ROWS]) | (lane == freshv[2, :, :ROWS])
    seen2 = jnp.concatenate([seen.astype(F32)] * 2, axis=0)
    fresh_w = weights_of(dot_t(my_q, g[q, 2])) * seen2
    suf_w = dot(fresh_w.astype(BF16), g[q, 3])
    suf_t = jnp.sum(fresh_w, axis=1, keepdims=True)
    for b in range(BEAMS):
        cached = weights_of(dot_t(my_q, kcv[b]))
        cached = jnp.where((anc2 == b) & in_use, cached, 0.0)
        suf_w = suf_w + dot(cached.astype(BF16), vcv[b])
        suf_t = suf_t + jnp.sum(cached, axis=1, keepdims=True)
    out_f[...] = g[q, 2:4]

    for h in range(2):
        both[h] = psend[0, h].astype(F32)
    for o in range(1, PN):
        p_copies[o].wait_recv()
        for h in range(2):
            both[h] += precv[o, h].astype(F32)
    theirs = both[1 - q]
    osend[pl.ds(0, QR), :] = theirs[:QR].astype(BF16)
    osend[pl.ds(QR, 16), :] = with_totals(theirs[QR : QR + 1] + theirs[QR + 8 : QR + 9])
    o_copy = push(rc(osend, orecv, os_, or_, across))
    ours = both[q]
    o_copy.wait_recv()
    ours = ours + orecv[...].astype(F32)
    line = ours[QR : QR + 1] + ours[QR + 8 : QR + 9]
    column = jnp.sum(jnp.where(eye, line, 0.0), axis=1, keepdims=True)
    attended = ((ours[:QR] + suf_w) / (column + suf_t)).astype(BF16)
    heads = jnp.concatenate([attended[:ROWS], attended[ROWS:]], axis=1)

    loc[0].wait()
    ordered = dot(perm[...], heads).astype(BF16)
    GRP = 4 * ZH
    HALF = YN * GRP
    wide = width // CHUNKS
    bc_copies = []
    for i in range(CHUNKS):
        for n in range(3):
            part = wide // 3
            at_col = pl.ds(i * wide + n * part, part)
            res = dot(ordered, woutv[:, at_col])
            for kk in range(KN):
                br[kk, i, :, pl.ds(n * part, part)] = res[kk * HALF : (kk + 1) * HALF]
        if KN > 1:
            csend[i] = br[1 - k, i].astype(BF16)
            bc_copies.append(push(rc(csend.at[i], crecv.at[i], bcs.at[i], bcr.at[i], at(k_=1 - k))))
    by_copies = {}
    for i in range(CHUNKS):
        total = br[k, i]
        if KN > 1:
            bc_copies[i].wait_recv()
            total = total + crecv[i].astype(F32)
        for yy in range(YN):
            s1[i, yy] = total[yy * GRP : (yy + 1) * GRP]
        for o in y_around:
            v = s1[i, y_of(o)]
            ysend[i, o] = jnp.concatenate([v[:, : wide // 2], v[:, wide // 2 :]], axis=0).astype(BF16)
            by_copies[i, o] = push(
                rc(ysend.at[i, o], yrecv.at[i, o], bys.at[i, o], byr.at[i, o], at(y_=y_of(o)))
            )
    bz_copies = []
    kept = []
    is_first = zh == 0
    quarter = wide // 4
    for i in range(CHUNKS):
        total = s1[i, y]
        for o in y_around:
            by_copies[i, o].wait_recv()
            v = yrecv[i, o].astype(F32)
            total = total + jnp.concatenate([v[:GRP], v[GRP:]], axis=1)
        if ZH > 1:
            other = jnp.where(is_first, total[4:8], total[0:4])
            zsend[i] = jnp.concatenate(
                [other[:, n * quarter : (n + 1) * quarter] for n in range(4)], axis=0
            ).astype(BF16)
            bz_copies.append(push(rc(zsend.at[i], zrecv.at[i], bzs.at[i], bzr.at[i], at(zh_=1 - zh))))
            kept.append(jnp.where(is_first, total[0:4], total[4:8]))
        else:
            kept.append(total[0:4])
    if ZH > 1:
        for i in range(CHUNKS):
            bz_copies[i].wait_recv()
            v = zrecv[i].astype(F32)
            kept[i] = kept[i] + jnp.concatenate([v[n * 4 : (n + 1) * 4] for n in range(4)], axis=1)
    square = sum(jnp.sum(v * v, axis=-1, keepdims=True) for v in kept) * (1.0 / width)
    factor = lax.rsqrt(square + epsilon)
    branch = jnp.concatenate(kept, axis=1) * factor
    out_h[...] = hid[...].astype(F32) + branch[:STEPS] * post_gain[...].reshape(1, width).astype(F32)

    for cp in sends:
        cp.wait_send()
    for to in range(XN):
        @pl.when(x != to)
        def _():
            w_copy(to).wait_send()


def cache_kernel(hid, fresh, kc, vc, par, lens, out_h, out_k, out_v, old, new, rows, ins, outs):
    beams, slots = kc.shape[0], kc.shape[1]
    length = lens[lax.axis_index("context")]
    loads = [pltpu.make_async_copy(src, old.at[i], ins.at[i]) for i, src in enumerate((kc, vc))]
    for cp in loads:
        cp.start()
    for t in range(STEPS):
        out_h[t, 0] = hid[t : t + 1]
    window = min(32, slots)
    start = pl.multiple_of(jnp.minimum(lax.div(length, 16) * 16, slots - window), 16)
    at_slot = iota((window, HEAD), 0) + start
    group = max(beams // 4, 1)
    stores = []
    for i, dst in enumerate((out_k, out_v)):
        rows[...] = fresh[i].astype(F32)
        loads[i].wait()
        for b in range(beams):
            two = par[2, 0, b]
            mid = par[1, 0, two]
            new[i, b] = old[i, par[0, 0, mid]]
            block = new[i, b, pl.ds(start, window), :].astype(F32)
            for u, row in enumerate((mid, two + beams, b + 2 * beams)):
                block = jnp.where(at_slot == length + u, rows[pl.ds(row, 1), :], block)
            new[i, b, pl.ds(start, window), :] = block.astype(BF16)
            if (b + 1) % group == 0:
                span = pl.ds(b + 1 - group, group)
                cp = pltpu.make_async_copy(new.at[i, span], dst.at[span], outs.at[i, b // group])
                cp.start()
                stores.append(cp)
    for cp in stores:
        cp.wait()


def order_matrix(dims):
    ZH, YN, KN, ZL = dims
    beams = ZH * YN * KN
    m = np.zeros((KN * YN * ZH * 4, STEPS * beams), np.float32)
    for kk in range(KN):
        for yy in range(YN):
            for hh in range(ZH):
                for t in range(STEPS):
                    m[((kk * YN + yy) * ZH + hh) * 4 + t, t * beams + (hh * YN + yy) * KN + kk] = 1.0
    return m


def body(
    dims,
    hidden_in,
    pre_gain,
    post_gain,
    w_query,
    key_projection_weight,
    value_projection_weight,
    w_out,
    prompt_rotated_keys,
    prompt_value_rows,
    suffix_key_cache,
    suffix_value_cache,
    parents,
    lengths,
):
    ZH, YN, KN, ZL = dims
    PN = ZL // 2
    GN = 2 * ZH
    YK = YN * KN
    beams = ZH * YK
    rows = STEPS * beams
    width = hidden_in.shape[3]
    slots = suffix_key_cache.shape[2]
    positions = prompt_rotated_keys.shape[0]
    prompt_total = positions * ZL * XN
    J = width // 256
    TJ = -(-(STEPS * J) // 16) * 16
    frequency = 1.0 / rope_base ** (np.arange(HEAD // 2) * 2.0 / HEAD)
    freq = jnp.asarray(np.concatenate([frequency, frequency])[None], F32)
    perm = jnp.asarray(order_matrix(dims), BF16)
    hbm = pl.BlockSpec(memory_space=pltpu.HBM)
    vmem = pl.BlockSpec(memory_space=pltpu.VMEM)
    smem = pl.BlockSpec(memory_space=pltpu.SMEM)
    wrows = w_query.shape[0]
    grp = 4 * ZH
    half = YN * grp
    wide = width // CHUNKS
    V = pltpu.VMEM
    D = pltpu.SemaphoreType.DMA
    scratch = [
        V((2, TJ, 128), BF16),
        V((2, TJ, 128), F32),
        V((2 * XN * STEPS, 128), F32),
        V((2 * XN * STEPS, 128), F32),
        V((GN, TJ, 128), BF16),
        V((GN * TJ, 128), F32),
        V((XN * YK, BLOCK, width // 2), BF16),
        V((PN, XN, wrows, HEAD), BF16),
        V((YK * BLOCK, HEAD), F32),
        V((XN, 2, rows, HEAD), BF16),
        V((XN, 2, rows, HEAD), BF16),
        V((2, XN, rows, HEAD), BF16),
        V((XN, 2, rows, HEAD), BF16),
        V((PN, 2, 2, rows, HEAD), BF16),
        V((XN, positions, HEAD), BF16),
        V((XN, positions, HEAD), BF16),
        V((4 * rows, 2 * HEAD), F32),
        V((PN, 2, 2 * rows + 16, HEAD), BF16),
        V((PN, 2, 2 * rows + 16, HEAD), BF16),
        V((2, 2 * rows + 16, HEAD), F32),
        V((2 * rows + 16, HEAD), BF16),
        V((2 * rows + 16, HEAD), BF16),
        V(w_out.shape, BF16),
        V((beams, slots, HEAD), BF16),
        V((beams, slots, HEAD), BF16),
        V((rows, 128), jnp.int32),
        V((STEPS, rows, 128), jnp.int32),
        V((KN, CHUNKS, half, wide), F32),
        V((CHUNKS, half, wide), BF16),
        V((CHUNKS, half, wide), BF16),
        V((CHUNKS, YN, grp, wide), F32),
        V((CHUNKS, YN, 2 * grp, wide // 2), BF16),
        V((CHUNKS, YN, 2 * grp, wide // 2), BF16),
        V((CHUNKS, 16, wide // 4), BF16),
        V((CHUNKS, 16, wide // 4), BF16),
        D((4,)), D((4,)), D((XN,)), D((XN,)), D((PN,)), D((PN,)), D((2, XN)), D((2, XN)),
        D((XN,)), D((XN,)), D((XN, 4)), D((XN, 4)), D((4,)), D((4,)), D((4, XN)), D((4, XN)),
        D((XN, 4)), D((XN, 4)), D((XN,)), D((XN,)), D((XN,)), D((XN,)), D((PN,)), D((PN,)),
        D((PN,)), D((PN,)), D, D, D((CHUNKS,)), D((CHUNKS,)), D((CHUNKS, 4)), D((CHUNKS, 4)),
        D((CHUNKS,)), D((CHUNKS,)), D((8,)),
    ]
    keys_in = suffix_key_cache.reshape(beams, slots, HEAD)
    values_in = suffix_value_cache.reshape(beams, slots, HEAD)
    hidden, fresh = pl.pallas_call(
        functools.partial(kernel, dims, prompt_total),
        out_shape=(
            jax.ShapeDtypeStruct((STEPS, width), F32),
            jax.ShapeDtypeStruct((2, rows, HEAD), BF16),
        ),
        in_specs=[vmem] * 5 + [hbm] * 8 + [smem] * 2,
        out_specs=(vmem, vmem),
        scratch_shapes=scratch,
        compiler_params=pltpu.CompilerParams(
            collective_id=0, has_side_effects=True, vmem_limit_bytes=63 * 1024 * 1024
        ),
    )(
        hidden_in.reshape(STEPS, width),
        pre_gain,
        post_gain,
        freq,
        perm,
        w_query,
        key_projection_weight,
        value_projection_weight,
        w_out,
        prompt_rotated_keys,
        prompt_value_rows,
        keys_in,
        values_in,
        parents,
        lengths,
    )
    hidden_out, keys_out, values_out = pl.pallas_call(
        cache_kernel,
        out_shape=(
            jax.ShapeDtypeStruct((STEPS, 1, 1, width), F32),
            jax.ShapeDtypeStruct((beams, slots, HEAD), BF16),
            jax.ShapeDtypeStruct((beams, slots, HEAD), BF16),
        ),
        in_specs=[vmem] * 2 + [hbm] * 2 + [smem] * 2,
        out_specs=(vmem, hbm, hbm),
        scratch_shapes=[
            V((2, beams, slots, HEAD), BF16),
            V((2, beams, slots, HEAD), BF16),
            V((rows, HEAD), F32),
            D((2,)),
            D((2, 4)),
        ],
        compiler_params=pltpu.CompilerParams(vmem_limit_bytes=63 * 1024 * 1024),
    )(hidden, fresh, keys_in, values_in, parents, lengths)
    return (
        hidden_out,
        keys_out.reshape(1, beams, slots, HEAD),
        values_out.reshape(1, beams, slots, HEAD),
    )


def solution(mesh, dims=(2, 4, 2, 8)):
    placed = (
        P(None, "context", "sample", None),
        P(),
        P(),
        P("context", "sample"),
        P("context", "sample"),
        P("context", "sample"),
        P("sample", None),
        P("context", "sample"),
        P("context", "sample"),
        P("context", None, None, "sample"),
        P("context", None, None, "sample"),
        P(None, "context", None),
        P(),
    )
    return jax.shard_map(
        functools.partial(body, dims),
        mesh=mesh,
        in_specs=placed,
        out_specs=(
            P(None, "context", "sample", None),
            P("context", None, None, "sample"),
            P("context", None, None, "sample"),
        ),
        check_vma=False,
    )
```

time: 105 us -> 104 us (level)
  local copies, waits for them, and re-layouts: 5.21 us -> 0 us
  Pallas kernels: 98 us -> 103 us
    unnamed x3 -> x0, local copies, waits for them, and re-layouts: 5.21 us -> none
    pallas_call x0 -> x1, Pallas kernels: none -> 3.7 us  [body(): pl.pallas_call(cache_kernel, out_shape=(jax.ShapeDtypeStruct((STEPS, 1, 1...]
    pallas_call x1, Pallas kernels: 98 us -> 99.2 us  [body(): pl.pallas_call(functools.partial(kernel, dims, prompt_total), out_shape=(...]
where the time goes in v3:
time: 104 us
  Pallas kernels  103 us (99%)
    pallas_call x1, Pallas kernels, body(): pl.pallas_call(functools.partial(kernel, dims, prompt_total), out_shape=(...  99.2 us
    pallas_call x1, Pallas kernels, body(): pl.pallas_call(cache_kernel, out_shape=(jax.ShapeDtypeStruct((STEPS, 1, 1...  3.7 us

profile of v3, /device:TPU:1, one launch (start us, length us, event | category | flops | bytes accessed | tf_op | source)
XLA Modules:
  0.0 103.5 jit_solution(5799690167777607184)
XLA Ops:
  0.6 99.2 %shard_map.166 = (f32[3,4608]{1,0:T(4,128)}, bf16[2,48,128]{2,1,0:T(8,128)(2,1)}) custom-call(bf16[3,4608]{1,0:T(4,128)(2,1)} %bitcast.9, bf16[4608]{0:T(1024)(128)(2,1)} %pre_gain.1, bf16[4608]{0:T(1024)(128)(2,1)} %post_gain.1, f32[1,128]{1,0:T(1,128)} %constant.4.clone.freq, bf16[64,48]{1,0:T(8,128)(2,1)} %constant.5.clone.perm, bf16[144,256]{1,0:T(8,128)(2,1)} %wq.1, ...), custom_call_target="tpu_custom_call" | custom-call | tf_op jit(solution)/shard_map/pallas_call | solution.py:632
  99.8 3.7 %shard_map.167 = (f32[3,1,1,4608]{3,2,1,0:T(1,128)}, bf16[16,128,128]{2,1,0:T(8,128)(2,1)}, bf16[16,128,128]{2,1,0:T(8,128)(2,1)}) custom-call(f32[3,4608]{1,0:T(4,128)} %get-tuple-element.8.hid, bf16[2,48,128]{2,1,0:T(8,128)(2,1)} %get-tuple-element.9.fresh, bf16[16,128,128]{2,1,0:T(8,128)(2,1)} %bitcast.6, bf16[16,128,128]{2,1,0:T(8,128)(2,1)} %bitcast.8, ...), custom_call_target="tpu_custom_call" | custom-call | tf_op jit(solution)/shard_map/pallas_call | solution.py:661

commit v4 on v3

--- a/solution.py
+++ b/solution.py
@@ -13,7 +13,6 @@
 XN = 4
 BLOCK = 16
 CHUNKS = 3
-POS_TILE = 512
 
 epsilon = 1e-06
 query_scale = 144.0 ** (-0.5)
@@ -172,11 +171,22 @@
         def _():
             w_local(to).start()
 
-    kv_copies = []
-
-    def send_prompt(which, o):
+    kv_copies = {}
+    positions = kall.shape[1]
+
+    def send_prompt(which, o, start=0, count=positions):
         src, dst = ((pk, kall), (pv, vall))[which]
-        kv_copies.append(push(rc(src, dst.at[x], ks.at[which, o], kr.at[which, o], at(x_=x_of(o)))))
+        span = pl.ds(start, count)
+        sem = 0 if start == 0 else 1
+        cp = rc(
+            src.at[span], dst.at[x, span], ks.at[which, o, sem], kr.at[which, o, sem], at(x_=x_of(o))
+        )
+        kv_copies.setdefault(o, []).append(push(cp))
+
+    for o in (1, 3):
+        send_prompt(0, o)
+    for o in (1, 3):
+        send_prompt(1, o, 0, positions // 2)
 
     a1[mine] = tiles[q]
     for to in range(XN):
@@ -192,8 +202,6 @@
         wz_copies.append(
             push(rc(wz.at[p], wz.at[p], wzs.at[o], wzr.at[o], at(zl_=q * PN + p_of(o))))
         )
-    send_prompt(0, 1)
-    send_prompt(0, 3)
     for cp in a_copies:
         cp.wait_recv()
 
@@ -279,6 +287,11 @@
                 sred[ox, h, pl.ds(t * BEAMS, BEAMS), :] = jnp.concatenate(piece, axis=0).astype(BF16)
         r_copies[ox] = push(rc(sred.at[ox], rred.at[ox], rs.at[ox], rr.at[ox], across))
 
+    for o in (1, 3):
+        send_prompt(1, o, positions // 2, positions // 2)
+    send_prompt(0, 2)
+    send_prompt(1, 2)
+
     gather(0)
     for cp in wz_copies:
         cp.wait_recv()
@@ -289,8 +302,6 @@
     gather(2)
     project(3)
     project(2)
-    for which, o in ((0, 2), (1, 1), (1, 3), (1, 2)):
-        send_prompt(which, o)
 
     NT = 2 * XN * STEPS
     at_row = iota((NT, 128), 0)
@@ -339,10 +350,6 @@
 
     for cp in loc[3:5]:
         cp.wait()
-    for cp in kv_copies:
-        cp.wait_recv()
-    per = kall.shape[1] // POS_TILE if kall.shape[1] >= POS_TILE else 1
-    tile = kall.shape[1] // per
     QR = 2 * ROWS
     eye = iota((QR, 128), 0) == iota((QR, 128), 1)
     upper = iota((16, 128), 0) < 8
@@ -356,18 +363,18 @@
         if o > 0:
             q_copies[o].wait_recv()
         there = p_of(-o)
-        acc[...] = jnp.zeros_like(acc)
-
-        def attend(i, carry):
-            xi = lax.div(i, per)
-            at_pos = pl.multiple_of(lax.rem(i, per) * tile, tile)
-            keys = kall[xi, pl.ds(at_pos, tile), :]
-            values = vall[xi, pl.ds(at_pos, tile), :]
-            w = weights_of(dot_t(qa[there].reshape(2 * QR, HEAD), keys)).astype(BF16)
-            acc[...] += dot(w, jnp.concatenate([values, jnp.ones((tile, HEAD), BF16)], axis=1))
-            return carry
-
-        lax.fori_loop(0, XN * per, attend, 0)
+        queries = qa[there].reshape(2 * QR, HEAD)
+        for ox in (0,) + AROUND:
+            if o == 0 and ox > 0:
+                for cp in kv_copies[ox]:
+                    cp.wait_recv()
+            xo = x_of(-ox)
+            w = weights_of(dot_t(queries, kall[xo])).astype(BF16)
+            part = dot(w, jnp.concatenate([vall[xo], jnp.ones((positions, HEAD), BF16)], axis=1))
+            if ox == 0:
+                acc[...] = part
+            else:
+                acc[...] += part
         for h in range(2):
             psend[o, h, pl.ds(0, QR), :] = acc[pl.ds(h * QR, QR), pl.ds(0, HEAD)].astype(BF16)
             totals = acc[pl.ds(h * QR, QR), pl.ds(HEAD, HEAD)]
@@ -621,7 +628,7 @@
         V((CHUNKS, YN, 2 * grp, wide // 2), BF16),
         V((CHUNKS, 16, wide // 4), BF16),
         V((CHUNKS, 16, wide // 4), BF16),
-        D((4,)), D((4,)), D((XN,)), D((XN,)), D((PN,)), D((PN,)), D((2, XN)), D((2, XN)),
+        D((4,)), D((4,)), D((XN,)), D((XN,)), D((PN,)), D((PN,)), D((2, XN, 2)), D((2, XN, 2)),
         D((XN,)), D((XN,)), D((XN, 4)), D((XN, 4)), D((4,)), D((4,)), D((4, XN)), D((4, XN)),
         D((XN, 4)), D((XN, 4)), D((XN,)), D((XN,)), D((XN,)), D((XN,)), D((PN,)), D((PN,)),
         D((PN,)), D((PN,)), D, D, D((CHUNKS,)), D((CHUNKS,)), D((CHUNKS, 4)), D((CHUNKS, 4)),

time: 104 us -> 92.4 us (0.89)
  Pallas kernels: 103 us -> 91.5 us
    pallas_call x1, Pallas kernels: 99.2 us -> 87.8 us  [body(): pl.pallas_call(functools.partial(kernel, dims, prompt_total), out_shape=(...]
where the time goes in v4:
time: 92.4 us; the launch traced here: 92.1 us
  Pallas kernels  91.5 us (99%)
    pallas_call x1, Pallas kernels, body(): pl.pallas_call(functools.partial(kernel, dims, prompt_total), out_shape=(...  87.8 us
    pallas_call x1, Pallas kernels, body(): pl.pallas_call(cache_kernel, out_shape=(jax.ShapeDtypeStruct((STEPS, 1, 1...  3.66 us

profile of v4, /device:TPU:1, one launch (start us, length us, event | category | flops | bytes accessed | tf_op | source)
XLA Modules:
  0.0 92.1 jit_solution(1568748674891029729)
XLA Ops:
  0.6 87.8 %shard_map.166 = (f32[3,4608]{1,0:T(4,128)}, bf16[2,48,128]{2,1,0:T(8,128)(2,1)}) custom-call(bf16[3,4608]{1,0:T(4,128)(2,1)} %bitcast.9, bf16[4608]{0:T(1024)(128)(2,1)} %pre_gain.1, bf16[4608]{0:T(1024)(128)(2,1)} %post_gain.1, f32[1,128]{1,0:T(1,128)} %constant.4.clone.freq, bf16[64,48]{1,0:T(8,128)(2,1)} %constant.5.clone.perm, bf16[144,256]{1,0:T(8,128)(2,1)} %wq.1, ...), custom_call_target="tpu_custom_call" | custom-call | tf_op jit(solution)/shard_map/pallas_call | solution.py:639
  88.5 3.7 %shard_map.167 = (f32[3,1,1,4608]{3,2,1,0:T(1,128)}, bf16[16,128,128]{2,1,0:T(8,128)(2,1)}, bf16[16,128,128]{2,1,0:T(8,128)(2,1)}) custom-call(f32[3,4608]{1,0:T(4,128)} %get-tuple-element.8.hid, bf16[2,48,128]{2,1,0:T(8,128)(2,1)} %get-tuple-element.9.fresh, bf16[16,128,128]{2,1,0:T(8,128)(2,1)} %bitcast.6, bf16[16,128,128]{2,1,0:T(8,128)(2,1)} %bitcast.8, ...), custom_call_target="tpu_custom_call" | custom-call | tf_op jit(solution)/shard_map/pallas_call | solution.py:668

commit v5 on v4

--- a/solution.py
+++ b/solution.py
@@ -46,8 +46,9 @@
 
 def kernel(
     dims, prompt_total,
-    hid, pre_gain, post_gain, freq, perm, wq, wk, wv, wout, pk, pv, kc, vc, par, lens,
+    hid_in, pre_in, post_in, freq_in, perm_in, wq, wk, wv, wout, pk, pv, kc, vc, par_in, lens_in,
     out_h, out_f,
+    hid, pre_gain, post_gain, freq, perm, par, lens,
     tiles, tilesf, cos_rows, sin_rows, a1, a1f, xb, wz, yf, sred, rred, g, gf, qa, kall, vall, acc,
     psend, precv, both, osend, orecv, woutv, kcv, vcv, ancv, freshv, br, csend, crecv, s1, ysend,
     yrecv, zsend, zrecv,
@@ -71,7 +72,7 @@
     z = zh * ZL + zl
     q = lax.div(zl, PN)
     p = lax.rem(zl, PN)
-    width = hid.shape[1]
+    width = hid_in.shape[1]
 
     def at(zh_=None, y_=None, k_=None, zl_=None, x_=None):
         zh_ = zh if zh_ is None else zh_
@@ -122,6 +123,15 @@
     for peer in peers:
         pl.semaphore_signal(barrier, inc=1, device_id=peer, device_id_type=MESH)
 
+    early = [pltpu.make_async_copy(hid_in, hid, ls.at[6]), pltpu.make_async_copy(pre_in, pre_gain, ls.at[7])]
+    late = [
+        pltpu.make_async_copy(src, dst, ls.at[8 + i])
+        for i, (src, dst) in enumerate(
+            ((post_in, post_gain), (freq_in, freq), (perm_in, perm), (par_in, par), (lens_in, lens))
+        )
+    ]
+    for cp in early + late:
+        cp.start()
     loc = [
         pltpu.make_async_copy(wout, woutv, ls.at[1]),
         pltpu.make_async_copy(kc, kcv, ls.at[2]),
@@ -134,6 +144,8 @@
 
     J = width // 256
     TJ = a1.shape[1]
+    for cp in early:
+        cp.wait()
     hid_f = hid[...].astype(F32)
     mean_square = jnp.mean(hid_f * hid_f, axis=-1, keepdims=True)
     normed = hid_f * lax.rsqrt(mean_square + epsilon) * pre_gain[...].reshape(1, width).astype(F32)
@@ -174,19 +186,27 @@
     kv_copies = {}
     positions = kall.shape[1]
 
-    def send_prompt(which, o, start=0, count=positions):
+    def send_prompt(which, o, part):
         src, dst = ((pk, kall), (pv, vall))[which]
-        span = pl.ds(start, count)
-        sem = 0 if start == 0 else 1
+        span = pl.ds(part * (positions // 2), positions // 2)
         cp = rc(
-            src.at[span], dst.at[x, span], ks.at[which, o, sem], kr.at[which, o, sem], at(x_=x_of(o))
+            src.at[span], dst.at[x, span], ks.at[which, o, part], kr.at[which, o, part], at(x_=x_of(o))
         )
-        kv_copies.setdefault(o, []).append(push(cp))
-
-    for o in (1, 3):
-        send_prompt(0, o)
-    for o in (1, 3):
-        send_prompt(1, o, 0, positions // 2)
+        kv_copies[which, o, part] = push(cp)
+
+    def pass_prompt(which, o):
+        part = 0 if o == 1 else 1
+        kv_copies.pop((which, o, part)).wait_recv()
+        block = (kall, vall)[which].at[x_of(-o), pl.ds(part * (positions // 2), positions // 2)]
+        cp = rc(block, block, ks.at[which, 2, part], kr.at[which, 2, part], at(x_=x_of(o)))
+        kv_copies[which, 2, part] = push(cp)
+
+    send_prompt(0, 1, 0)
+    send_prompt(0, 3, 1)
+    send_prompt(1, 1, 0)
+    send_prompt(1, 3, 1)
+    send_prompt(0, 1, 1)
+    send_prompt(0, 3, 0)
 
     a1[mine] = tiles[q]
     for to in range(XN):
@@ -287,10 +307,11 @@
                 sred[ox, h, pl.ds(t * BEAMS, BEAMS), :] = jnp.concatenate(piece, axis=0).astype(BF16)
         r_copies[ox] = push(rc(sred.at[ox], rred.at[ox], rs.at[ox], rr.at[ox], across))
 
-    for o in (1, 3):
-        send_prompt(1, o, positions // 2, positions // 2)
-    send_prompt(0, 2)
-    send_prompt(1, 2)
+    for which in range(2):
+        for o in (1, 3):
+            pass_prompt(which, o)
+    send_prompt(1, 1, 1)
+    send_prompt(1, 3, 0)
 
     gather(0)
     for cp in wz_copies:
@@ -303,6 +324,8 @@
     project(3)
     project(2)
 
+    for cp in late:
+        cp.wait()
     NT = 2 * XN * STEPS
     at_row = iota((NT, 128), 0)
     place = jnp.zeros((NT, 128), jnp.int32)
@@ -366,8 +389,9 @@
         queries = qa[there].reshape(2 * QR, HEAD)
         for ox in (0,) + AROUND:
             if o == 0 and ox > 0:
-                for cp in kv_copies[ox]:
-                    cp.wait_recv()
+                for key, cp in kv_copies.items():
+                    if key[1] == ox:
+                        cp.wait_recv()
             xo = x_of(-ox)
             w = weights_of(dot_t(queries, kall[xo])).astype(BF16)
             part = dot(w, jnp.concatenate([vall[xo], jnp.ones((positions, HEAD), BF16)], axis=1))
@@ -446,7 +470,9 @@
     HALF = YN * GRP
     wide = width // CHUNKS
     bc_copies = []
-    for i in range(CHUNKS):
+    by_copies = {}
+
+    def project_out(i):
         for n in range(3):
             part = wide // 3
             at_col = pl.ds(i * wide + n * part, part)
@@ -456,20 +482,26 @@
         if KN > 1:
             csend[i] = br[1 - k, i].astype(BF16)
             bc_copies.append(push(rc(csend.at[i], crecv.at[i], bcs.at[i], bcr.at[i], at(k_=1 - k))))
-    by_copies = {}
-    for i in range(CHUNKS):
+
+    def over_y(i):
         total = br[k, i]
         if KN > 1:
             bc_copies[i].wait_recv()
             total = total + crecv[i].astype(F32)
         for yy in range(YN):
             s1[i, yy] = total[yy * GRP : (yy + 1) * GRP]
-        for o in y_around:
+        for o in reversed(y_around):
             v = s1[i, y_of(o)]
             ysend[i, o] = jnp.concatenate([v[:, : wide // 2], v[:, wide // 2 :]], axis=0).astype(BF16)
             by_copies[i, o] = push(
                 rc(ysend.at[i, o], yrecv.at[i, o], bys.at[i, o], byr.at[i, o], at(y_=y_of(o)))
             )
+
+    project_out(0)
+    for i in range(1, CHUNKS):
+        project_out(i)
+        over_y(i - 1)
+    over_y(CHUNKS - 1)
     bz_copies = []
     kept = []
     is_first = zh == 0
@@ -497,7 +529,9 @@
     square = sum(jnp.sum(v * v, axis=-1, keepdims=True) for v in kept) * (1.0 / width)
     factor = lax.rsqrt(square + epsilon)
     branch = jnp.concatenate(kept, axis=1) * factor
-    out_h[...] = hid[...].astype(F32) + branch[:STEPS] * post_gain[...].reshape(1, width).astype(F32)
+    result = hid[...].astype(F32) + branch[:STEPS] * post_gain[...].reshape(1, width).astype(F32)
+    for t in range(STEPS):
+        out_h[t, 0] = result[t : t + 1]
 
     for cp in sends:
         cp.wait_send()
@@ -507,21 +541,24 @@
             w_copy(to).wait_send()
 
 
-def cache_kernel(hid, fresh, kc, vc, par, lens, out_h, out_k, out_v, old, new, rows, ins, outs):
+def cache_kernel(
+    hid, fresh, kc, vc, par, lens, out_h, out_k, out_v, hidv, freshv, old, new, rows, ins, outs, sem
+):
     beams, slots = kc.shape[0], kc.shape[1]
+    loads = [pltpu.make_async_copy(src, old.at[i], ins.at[i]) for i, src in enumerate((kc, vc))]
+    loads.append(pltpu.make_async_copy(fresh, freshv, ins.at[2]))
+    loads.append(pltpu.make_async_copy(hid, hidv, ins.at[3]))
+    for i in (2, 0, 1, 3):
+        loads[i].start()
     length = lens[lax.axis_index("context")]
-    loads = [pltpu.make_async_copy(src, old.at[i], ins.at[i]) for i, src in enumerate((kc, vc))]
-    for cp in loads:
-        cp.start()
-    for t in range(STEPS):
-        out_h[t, 0] = hid[t : t + 1]
     window = min(32, slots)
     start = pl.multiple_of(jnp.minimum(lax.div(length, 16) * 16, slots - window), 16)
     at_slot = iota((window, HEAD), 0) + start
     group = max(beams // 4, 1)
     stores = []
+    loads[2].wait()
     for i, dst in enumerate((out_k, out_v)):
-        rows[...] = fresh[i].astype(F32)
+        rows[...] = freshv[i].astype(F32)
         loads[i].wait()
         for b in range(beams):
             two = par[2, 0, b]
@@ -536,6 +573,11 @@
                 cp = pltpu.make_async_copy(new.at[i, span], dst.at[span], outs.at[i, b // group])
                 cp.start()
                 stores.append(cp)
+        if i == 0:
+            loads[3].wait()
+            cp = pltpu.make_async_copy(hidv, out_h, sem)
+            cp.start()
+            stores.append(cp)
     for cp in stores:
         cp.wait()
 
@@ -593,6 +635,13 @@
     V = pltpu.VMEM
     D = pltpu.SemaphoreType.DMA
     scratch = [
+        V((STEPS, width), BF16),
+        V((width,), BF16),
+        V((width,), BF16),
+        V((1, HEAD), F32),
+        V(perm.shape, BF16),
+        pltpu.SMEM(parents.shape, jnp.int32),
+        pltpu.SMEM(lengths.shape, jnp.int32),
         V((2, TJ, 128), BF16),
         V((2, TJ, 128), F32),
         V((2 * XN * STEPS, 128), F32),
@@ -632,17 +681,17 @@
         D((XN,)), D((XN,)), D((XN, 4)), D((XN, 4)), D((4,)), D((4,)), D((4, XN)), D((4, XN)),
         D((XN, 4)), D((XN, 4)), D((XN,)), D((XN,)), D((XN,)), D((XN,)), D((PN,)), D((PN,)),
         D((PN,)), D((PN,)), D, D, D((CHUNKS,)), D((CHUNKS,)), D((CHUNKS, 4)), D((CHUNKS, 4)),
-        D((CHUNKS,)), D((CHUNKS,)), D((8,)),
+        D((CHUNKS,)), D((CHUNKS,)), D((16,)),
     ]
     keys_in = suffix_key_cache.reshape(beams, slots, HEAD)
     values_in = suffix_value_cache.reshape(beams, slots, HEAD)
     hidden, fresh = pl.pallas_call(
         functools.partial(kernel, dims, prompt_total),
         out_shape=(
-            jax.ShapeDtypeStruct((STEPS, width), F32),
+            jax.ShapeDtypeStruct((STEPS, 1, 1, width), F32),
             jax.ShapeDtypeStruct((2, rows, HEAD), BF16),
         ),
-        in_specs=[vmem] * 5 + [hbm] * 8 + [smem] * 2,
+        in_specs=[hbm] * 15,
         out_specs=(vmem, vmem),
         scratch_shapes=scratch,
         compiler_params=pltpu.CompilerParams(
@@ -672,14 +721,17 @@
             jax.ShapeDtypeStruct((beams, slots, HEAD), BF16),
             jax.ShapeDtypeStruct((beams, slots, HEAD), BF16),
         ),
-        in_specs=[vmem] * 2 + [hbm] * 2 + [smem] * 2,
-        out_specs=(vmem, hbm, hbm),
+        in_specs=[hbm] * 4 + [smem] * 2,
+        out_specs=(hbm, hbm, hbm),
         scratch_shapes=[
+            V((STEPS, 1, 1, width), F32),
+            V((2, rows, HEAD), BF16),
             V((2, beams, slots, HEAD), BF16),
             V((2, beams, slots, HEAD), BF16),
             V((rows, HEAD), F32),
-            D((2,)),
+            D((4,)),
             D((2, 4)),
+            D,
         ],
         compiler_params=pltpu.CompilerParams(vmem_limit_bytes=63 * 1024 * 1024),
     )(hidden, fresh, keys_in, values_in, parents, lengths)

time: 92.4 us -> 87.2 us (0.944)
  Pallas kernels: 91.5 us -> 86.4 us
    pallas_call x1, Pallas kernels: 87.8 us -> 83.4 us  [body(): pl.pallas_call(functools.partial(kernel, dims, prompt_total), out_shape=(...]
where the time goes in v5:
time: 87.2 us; the launch traced here: 87 us
  Pallas kernels  86.4 us (99%)
    pallas_call x1, Pallas kernels, body(): pl.pallas_call(functools.partial(kernel, dims, prompt_total), out_shape=(...  83.4 us
    pallas_call x1, Pallas kernels, body(): pl.pallas_call(cache_kernel, out_shape=(jax.ShapeDtypeStruct((STEPS, 1, 1...  2.92 us

profile of v5, /device:TPU:1, one launch (start us, length us, event | category | flops | bytes accessed | tf_op | source)
XLA Modules:
  0.0 87.0 jit_solution(17480746403184641898)
XLA Ops:
  0.6 83.4 %shard_map.166 = (f32[3,1,1,4608]{3,2,1,0:T(1,128)}, bf16[2,48,128]{2,1,0:T(8,128)(2,1)}) custom-call(bf16[3,4608]{1,0:T(4,128)(2,1)} %bitcast.9, bf16[4608]{0:T(1024)(128)(2,1)} %pre_in.1, bf16[4608]{0:T(1024)(128)(2,1)} %post_in.1, f32[1,128]{1,0:T(1,128)} %constant.4.clone.freq_in, bf16[64,48]{1,0:T(8,128)(2,1)} %constant.5.clone.perm_in, ...), custom_call_target="tpu_custom_call" | custom-call | tf_op jit(solution)/shard_map/pallas_call | solution.py:688
  84.1 2.9 %shard_map.167 = (f32[3,1,1,4608]{3,2,1,0:T(1,128)}, bf16[16,128,128]{2,1,0:T(8,128)(2,1)}, bf16[16,128,128]{2,1,0:T(8,128)(2,1)}) custom-call(f32[3,1,1,4608]{3,2,1,0:T(1,128)} %get-tuple-element.8.hid, bf16[2,48,128]{2,1,0:T(8,128)(2,1)} %get-tuple-element.9.fresh, bf16[16,128,128]{2,1,0:T(8,128)(2,1)} %bitcast.6, bf16[16,128,128]{2,1,0:T(8,128)(2,1)} %bitcast.8, ...), custom_call_target="tpu_custom_call" | custom-call | tf_op jit(solution)/shard_map/pallas_call | solution.py:717

commit v6 on v5

--- a/solution.py
+++ b/solution.py
@@ -49,10 +49,10 @@
     hid_in, pre_in, post_in, freq_in, perm_in, wq, wk, wv, wout, pk, pv, kc, vc, par_in, lens_in,
     out_h, out_f,
     hid, pre_gain, post_gain, freq, perm, par, lens,
-    tiles, tilesf, cos_rows, sin_rows, a1, a1f, xb, wz, yf, sred, rred, g, gf, qa, kall, vall, acc,
+    tiles, relay, tilesf, cos_rows, sin_rows, a1, a1f, xb, wz, yf, sred, rred, g, gf, qa, kall, vall, acc,
     psend, precv, both, osend, orecv, woutv, kcv, vcv, ancv, freshv, br, csend, crecv, s1, ysend,
     yrecv, zsend, zrecv,
-    as_, ar, ws, wr, wzs, wzr, ks, kr, pxs, pxr, pys, pyr, rys, ryr, rxs, rxr, cs, cr, rs, rr, gs,
+    as_, ar, hs, hr, fs, fr, ws, wr, wzs, wzr, ks, kr, pxs, pxr, pys, pyr, rys, ryr, rxs, rxr, cs, cr, rs, rr, gs,
     gr, qs, qr, ps, pr, os_, or_, bcs, bcr, bys, byr, bzs, bzr, ls,
 ):
     ZH, YN, KN, ZL = dims
@@ -111,14 +111,12 @@
 
     across = at(zl_=(1 - q) * PN + p)
 
-    peers = [half_at(m)[0] for m in range(1, GN)]
+    peers = [half_at(m)[0] for m in range(1, GN, 2)]
     peers += [at(zl_=q * PN + p_of(o)) for o in range(1, PN)]
     peers += [at(x_=x_of(o)) for o in range(1, XN)]
     peers += [at(y_=y_of(o)) for o in range(1, YN)]
     if KN > 1:
         peers += [at(k_=1 - k)]
-    if ZH == 1:
-        assert GN == 2
     barrier = pltpu.get_barrier_semaphore()
     for peer in peers:
         pl.semaphore_signal(barrier, inc=1, device_id=peer, device_id_type=MESH)
@@ -160,10 +158,15 @@
 
     mine = lax.div(z, PN)
     a_copies = []
-    for m in (2, 1, 3):
-        if m < GN:
-            where, q_to = half_at(m)
-            a_copies.append(push(rc(tiles.at[q_to], a1.at[mine], as_.at[m], ar.at[m], where)))
+    h_copies = []
+    TH = TJ // 2
+    if GN > 2:
+        for i, m in enumerate((1, 3)):
+            part = tiles.at[q, pl.ds(i * TH, TH)]
+            h_copies.append(push(rc(part, relay.at[i], hs.at[i], hr.at[i], half_at(m)[0])))
+    for m in range(1, GN, 2):
+        where, q_to = half_at(m)
+        a_copies.append(push(rc(tiles.at[q_to], a1.at[mine], as_.at[m], ar.at[m], where)))
 
     half = wq.shape[1] // 2
     w_src = [wq.at[:, pl.ds(0, half)], wq.at[:, pl.ds(half, half)], wk, wv]
@@ -209,6 +212,10 @@
     send_prompt(0, 3, 0)
 
     a1[mine] = tiles[q]
+    for i, cp in enumerate(h_copies):
+        cp.wait_recv()
+        target = a1.at[lax.rem(mine + (GN - 1, 1)[i], GN), pl.ds(i * TH, TH)]
+        a_copies.append(push(rc(relay.at[i], target, fs.at[i], fr.at[i], half_at((1, 3)[i])[0])))
     for to in range(XN):
         @pl.when(x != to)
         def _():
@@ -643,6 +650,7 @@
         pltpu.SMEM(parents.shape, jnp.int32),
         pltpu.SMEM(lengths.shape, jnp.int32),
         V((2, TJ, 128), BF16),
+        V((2, TJ // 2, 128), BF16),
         V((2, TJ, 128), F32),
         V((2 * XN * STEPS, 128), F32),
         V((2 * XN * STEPS, 128), F32),
@@ -677,7 +685,7 @@
         V((CHUNKS, YN, 2 * grp, wide // 2), BF16),
         V((CHUNKS, 16, wide // 4), BF16),
         V((CHUNKS, 16, wide // 4), BF16),
-        D((4,)), D((4,)), D((XN,)), D((XN,)), D((PN,)), D((PN,)), D((2, XN, 2)), D((2, XN, 2)),
+        D((4,)), D((4,)), D((2,)), D((2,)), D((2,)), D((2,)), D((XN,)), D((XN,)), D((PN,)), D((PN,)), D((2, XN, 2)), D((2, XN, 2)),
         D((XN,)), D((XN,)), D((XN, 4)), D((XN, 4)), D((4,)), D((4,)), D((4, XN)), D((4, XN)),
         D((XN, 4)), D((XN, 4)), D((XN,)), D((XN,)), D((XN,)), D((XN,)), D((PN,)), D((PN,)),
         D((PN,)), D((PN,)), D, D, D((CHUNKS,)), D((CHUNKS,)), D((CHUNKS, 4)), D((CHUNKS, 4)),

time: 87.2 us -> 86.9 us (level)
  no operation moved by 1% of the time
where the time goes in v6:
time: 86.9 us; the launch traced here: 86.8 us
  Pallas kernels  86.1 us (99%)
    pallas_call x1, Pallas kernels, body(): pl.pallas_call(functools.partial(kernel, dims, prompt_total), out_shape=(...  83.2 us
    pallas_call x1, Pallas kernels, body(): pl.pallas_call(cache_kernel, out_shape=(jax.ShapeDtypeStruct((STEPS, 1, 1...  2.92 us

profile of v6, /device:TPU:1, one launch (start us, length us, event | category | flops | bytes accessed | tf_op | source)
XLA Modules:
  0.0 86.8 jit_solution(6188703222429763642)
XLA Ops:
  0.6 83.2 %shard_map.166 = (f32[3,1,1,4608]{3,2,1,0:T(1,128)}, bf16[2,48,128]{2,1,0:T(8,128)(2,1)}) custom-call(bf16[3,4608]{1,0:T(4,128)(2,1)} %bitcast.9, bf16[4608]{0:T(1024)(128)(2,1)} %pre_in.1, bf16[4608]{0:T(1024)(128)(2,1)} %post_in.1, f32[1,128]{1,0:T(1,128)} %constant.4.clone.freq_in, bf16[64,48]{1,0:T(8,128)(2,1)} %constant.5.clone.perm_in, ...), custom_call_target="tpu_custom_call" | custom-call | tf_op jit(solution)/shard_map/pallas_call | solution.py:696
  83.8 2.9 %shard_map.167 = (f32[3,1,1,4608]{3,2,1,0:T(1,128)}, bf16[16,128,128]{2,1,0:T(8,128)(2,1)}, bf16[16,128,128]{2,1,0:T(8,128)(2,1)}) custom-call(f32[3,1,1,4608]{3,2,1,0:T(1,128)} %get-tuple-element.8.hid, bf16[2,48,128]{2,1,0:T(8,128)(2,1)} %get-tuple-element.9.fresh, bf16[16,128,128]{2,1,0:T(8,128)(2,1)} %bitcast.6, bf16[16,128,128]{2,1,0:T(8,128)(2,1)} %bitcast.8, ...), custom_call_target="tpu_custom_call" | custom-call | tf_op jit(solution)/shard_map/pallas_call | solution.py:725

commit v7 on v6

--- a/solution.py
+++ b/solution.py
@@ -49,10 +49,10 @@
     hid_in, pre_in, post_in, freq_in, perm_in, wq, wk, wv, wout, pk, pv, kc, vc, par_in, lens_in,
     out_h, out_f,
     hid, pre_gain, post_gain, freq, perm, par, lens,
-    tiles, relay, tilesf, cos_rows, sin_rows, a1, a1f, xb, wz, yf, sred, rred, g, gf, qa, kall, vall, acc,
+    tiles, relay, tilesf, cos_rows, sin_rows, a1, a1f, xb, wz, yk, ysnd, ystd, sred, rred, g, gf, qa, kall, vall, acc,
     psend, precv, both, osend, orecv, woutv, kcv, vcv, ancv, freshv, br, csend, crecv, s1, ysend,
     yrecv, zsend, zrecv,
-    as_, ar, hs, hr, fs, fr, ws, wr, wzs, wzr, ks, kr, pxs, pxr, pys, pyr, rys, ryr, rxs, rxr, cs, cr, rs, rr, gs,
+    as_, ar, hs, hr, fs, fr, ws, wr, wzs, wzr, wcs, wcr, ks, kr, pxs, pxr, pys, pyr, rys, ryr, rxs, rxr, cs, cr, rs, rr, gs,
     gr, qs, qr, ps, pr, os_, or_, bcs, bcr, bys, byr, bzs, bzr, ls,
 ):
     ZH, YN, KN, ZL = dims
@@ -111,6 +111,16 @@
 
     across = at(zl_=(1 - q) * PN + p)
 
+    early = [pltpu.make_async_copy(hid_in, hid, ls.at[6]), pltpu.make_async_copy(pre_in, pre_gain, ls.at[7])]
+    late = [
+        pltpu.make_async_copy(src, dst, ls.at[8 + i])
+        for i, (src, dst) in enumerate(
+            ((post_in, post_gain), (freq_in, freq), (perm_in, perm), (par_in, par), (lens_in, lens))
+        )
+    ]
+    for cp in early:
+        cp.start()
+
     peers = [half_at(m)[0] for m in range(1, GN, 2)]
     peers += [at(zl_=q * PN + p_of(o)) for o in range(1, PN)]
     peers += [at(x_=x_of(o)) for o in range(1, XN)]
@@ -121,15 +131,6 @@
     for peer in peers:
         pl.semaphore_signal(barrier, inc=1, device_id=peer, device_id_type=MESH)
 
-    early = [pltpu.make_async_copy(hid_in, hid, ls.at[6]), pltpu.make_async_copy(pre_in, pre_gain, ls.at[7])]
-    late = [
-        pltpu.make_async_copy(src, dst, ls.at[8 + i])
-        for i, (src, dst) in enumerate(
-            ((post_in, post_gain), (freq_in, freq), (perm_in, perm), (par_in, par), (lens_in, lens))
-        )
-    ]
-    for cp in early + late:
-        cp.start()
     loc = [
         pltpu.make_async_copy(wout, woutv, ls.at[1]),
         pltpu.make_async_copy(kc, kcv, ls.at[2]),
@@ -137,7 +138,7 @@
         pltpu.make_async_copy(pk, kall.at[x], ls.at[4]),
         pltpu.make_async_copy(pv, vall.at[x], ls.at[5]),
     ]
-    for cp in loc:
+    for cp in late + loc:
         cp.start()
 
     J = width // 256
@@ -171,11 +172,14 @@
     half = wq.shape[1] // 2
     w_src = [wq.at[:, pl.ds(0, half)], wq.at[:, pl.ds(half, half)], wk, wv]
 
+    def own_part(x_):
+        return wz.at[p, x_, :, pl.ds(0, HEAD)]
+
     def w_copy(to):
-        return rc(w_src[to], wz.at[p, x], ws.at[to], wr.at[x], at(x_=to))
+        return rc(w_src[to], own_part(x), ws.at[to], wr.at[x], at(x_=to))
 
     def w_local(to):
-        return pltpu.make_async_copy(w_src[to], wz.at[p, x], ls.at[0])
+        return pltpu.make_async_copy(w_src[to], own_part(x), ls.at[0])
 
     for to in range(XN):
         @pl.when(x != to)
@@ -219,22 +223,32 @@
     for to in range(XN):
         @pl.when(x != to)
         def _():
-            rc(w_src[to], wz.at[p, to], ws.at[to], wr.at[to], at(x_=to)).wait_recv()
+            rc(w_src[to], own_part(to), ws.at[to], wr.at[to], at(x_=to)).wait_recv()
 
         @pl.when(x == to)
         def _():
             w_local(to).wait()
-    wz_copies = []
+    wz_copies = {}
+    wc_copies = []
     for o in range(1, PN):
-        wz_copies.append(
-            push(rc(wz.at[p], wz.at[p], wzs.at[o], wzr.at[o], at(zl_=q * PN + p_of(o))))
-        )
+        part = wz.at[p, :, :, pl.ds(0, HEAD)]
+        wz_copies[o] = push(rc(part, part, wzs.at[o], wzr.at[o], at(zl_=q * PN + p_of(o))))
+
+    def weights_to_core(o):
+        if o > 0:
+            wz_copies[o].wait_recv()
+        if KN > 1:
+            from_ = wz.at[p_of(-o), :, :, pl.ds(0, HEAD)]
+            into = wz.at[p_of(-o), :, :, pl.ds(HEAD, HEAD)]
+            wc_copies.append(push(rc(from_, into, wcs.at[o], wcr.at[o], at(k_=1 - k))))
+
+    weights_to_core(0)
     for cp in a_copies:
         cp.wait_recv()
 
     for i in range(GN):
         a1f[pl.ds(i * TJ, TJ), :] = a1[i].astype(F32)
-    own = (x * YN + y) * KN + k
+    own = x * YN + y
     rest = jnp.zeros((BLOCK - STEPS * GN, 128), F32)
     for j in range(J):
         lines = [a1f[pl.ds(j * STEPS + t, GN, stride=TJ), :] for t in range(STEPS)]
@@ -243,7 +257,7 @@
     cols = xb.shape[2] // 2
 
     def blk(ox, oy):
-        return (x_of(-ox) * YN + y_of(-oy)) * KN + k
+        return x_of(-ox) * YN + y_of(-oy)
 
     def first(b):
         return xb.at[b, :, pl.ds(0, cols)]
@@ -262,11 +276,6 @@
         b = blk(0, oy)
         for o in AROUND:
             rx[oy, o] = push(rc(second(b), second(b), rxs.at[oy, o], rxr.at[oy, o], at(x_=x_of(o))))
-
-    def to_core(ox, oy):
-        if KN > 1:
-            b = xb.at[blk(ox, oy)]
-            cc[ox, oy] = push(rc(b, b, cs.at[ox, oy], cr.at[ox, oy], at(k_=1 - k)))
 
     y_around = [o for o in AROUND if o < YN]
     for o in AROUND:
@@ -279,7 +288,6 @@
             b = blk(0, 0)
             py[0, o] = push(rc(first(b), first(b), pys.at[0, o], pyr.at[0, o], at(y_=y_of(o))))
     forward_x(0)
-    to_core(0, 0)
     for o in AROUND:
         px[o].wait_recv()
         for o2 in y_around:
@@ -295,23 +303,28 @@
                 py[ox, oy].wait_recv()
             if ox > 0:
                 rx[oy, ox].wait_recv()
-            if ox > 0 or oy > 0:
-                to_core(ox, oy)
 
     r_copies = {}
 
     def project(ox):
-        for oy in [0] + y_around:
-            if KN > 1:
-                cc[ox, oy].wait_recv()
-        rows = xb[pl.ds(x_of(-ox) * YK, YK)].reshape(YK * BLOCK, xb.shape[2])
-        yf[...] = dot(rows, wz[...].reshape(xb.shape[2], HEAD))
-        for h in range(2):
-            for t in range(STEPS):
-                piece = [
-                    yf[pl.ds(t * GN + i * 2 + h, YK, stride=BLOCK), :] for i in range(ZH)
-                ]
-                sred[ox, h, pl.ds(t * BEAMS, BEAMS), :] = jnp.concatenate(piece, axis=0).astype(BF16)
+        rows = xb[pl.ds(x_of(-ox) * YN, YN)].reshape(YN * BLOCK, xb.shape[2])
+        res = dot(rows, wz[...].reshape(xb.shape[2], KN * HEAD))
+        yk[ox, k] = res[:, :HEAD]
+        if KN > 1:
+            ysnd[ox] = res[:, HEAD:]
+            cc[ox] = push(rc(ysnd.at[ox], yk.at[ox, k], cs.at[ox], cr.at[ox], at(k_=1 - k)))
+
+    def finish(ox):
+        if KN > 1:
+            cc[ox].wait_recv()
+        for kk in range(KN):
+            for h in range(2):
+                for t in range(STEPS):
+                    for i in range(ZH):
+                        lines = yk[ox, kk, pl.ds(t * GN + i * 2 + h, YN, stride=BLOCK), :]
+                        start = h * ROWS + t * BEAMS + i * YK + kk
+                        ystd[pl.ds(start, YN, stride=KN), :] = lines
+        sred[ox] = ystd[...].reshape(2, ROWS, HEAD).astype(BF16)
         r_copies[ox] = push(rc(sred.at[ox], rred.at[ox], rs.at[ox], rr.at[ox], across))
 
     for which in range(2):
@@ -320,16 +333,22 @@
     send_prompt(1, 1, 1)
     send_prompt(1, 3, 0)
 
+    for o in [o for o in AROUND if o < PN]:
+        weights_to_core(o)
     gather(0)
-    for cp in wz_copies:
+    for cp in wc_copies:
         cp.wait_recv()
     project(0)
     gather(1)
+    project(1)
+    finish(0)
     gather(3)
-    project(1)
+    project(3)
+    finish(1)
     gather(2)
-    project(3)
     project(2)
+    finish(3)
+    finish(2)
 
     for cp in late:
         cp.wait()
@@ -656,9 +675,11 @@
         V((2 * XN * STEPS, 128), F32),
         V((GN, TJ, 128), BF16),
         V((GN * TJ, 128), F32),
-        V((XN * YK, BLOCK, width // 2), BF16),
-        V((PN, XN, wrows, HEAD), BF16),
-        V((YK * BLOCK, HEAD), F32),
+        V((XN * YN, BLOCK, width // 2), BF16),
+        V((PN, XN, wrows, KN * HEAD), BF16),
+        V((XN, KN, YN * BLOCK, HEAD), F32),
+        V((XN, YN * BLOCK, HEAD), F32),
+        V((2 * rows, HEAD), F32),
         V((XN, 2, rows, HEAD), BF16),
         V((XN, 2, rows, HEAD), BF16),
         V((2, XN, rows, HEAD), BF16),
@@ -685,9 +706,9 @@
         V((CHUNKS, YN, 2 * grp, wide // 2), BF16),
         V((CHUNKS, 16, wide // 4), BF16),
         V((CHUNKS, 16, wide // 4), BF16),
-        D((4,)), D((4,)), D((2,)), D((2,)), D((2,)), D((2,)), D((XN,)), D((XN,)), D((PN,)), D((PN,)), D((2, XN, 2)), D((2, XN, 2)),
+        D((4,)), D((4,)), D((2,)), D((2,)), D((2,)), D((2,)), D((XN,)), D((XN,)), D((PN,)), D((PN,)), D((PN,)), D((PN,)), D((2, XN, 2)), D((2, XN, 2)),
         D((XN,)), D((XN,)), D((XN, 4)), D((XN, 4)), D((4,)), D((4,)), D((4, XN)), D((4, XN)),
-        D((XN, 4)), D((XN, 4)), D((XN,)), D((XN,)), D((XN,)), D((XN,)), D((PN,)), D((PN,)),
+        D((XN,)), D((XN,)), D((XN,)), D((XN,)), D((XN,)), D((XN,)), D((PN,)), D((PN,)),
         D((PN,)), D((PN,)), D, D, D((CHUNKS,)), D((CHUNKS,)), D((CHUNKS, 4)), D((CHUNKS, 4)),
         D((CHUNKS,)), D((CHUNKS,)), D((16,)),
     ]

time: 86.9 us -> 88.5 us (1.018)
  Pallas kernels: 86.1 us -> 87.6 us
    pallas_call x1, Pallas kernels: 83.2 us -> 84.8 us  [body(): pl.pallas_call(functools.partial(kernel, dims, prompt_total), out_shape=(...]
where the time goes in v7:
time: 88.5 us; the launch traced here: 88.3 us
  Pallas kernels  87.6 us (99%)
    pallas_call x1, Pallas kernels, body(): pl.pallas_call(functools.partial(kernel, dims, prompt_total), out_shape=(...  84.8 us
    pallas_call x1, Pallas kernels, body(): pl.pallas_call(cache_kernel, out_shape=(jax.ShapeDtypeStruct((STEPS, 1, 1...  2.89 us

profile of v7, /device:TPU:1, one launch (start us, length us, event | category | flops | bytes accessed | tf_op | source)
XLA Modules:
  0.0 88.3 jit_solution(5932737699075300073)
XLA Ops:
  0.6 84.8 %shard_map.166 = (f32[3,1,1,4608]{3,2,1,0:T(1,128)}, bf16[2,48,128]{2,1,0:T(8,128)(2,1)}) custom-call(bf16[3,4608]{1,0:T(4,128)(2,1)} %bitcast.9, bf16[4608]{0:T(1024)(128)(2,1)} %pre_in.1, bf16[4608]{0:T(1024)(128)(2,1)} %post_in.1, f32[1,128]{1,0:T(1,128)} %constant.4.clone.freq_in, bf16[64,48]{1,0:T(8,128)(2,1)} %constant.5.clone.perm_in, ...), custom_call_target="tpu_custom_call" | custom-call | tf_op jit(solution)/shard_map/pallas_call | solution.py:717
  85.4 2.9 %shard_map.167 = (f32[3,1,1,4608]{3,2,1,0:T(1,128)}, bf16[16,128,128]{2,1,0:T(8,128)(2,1)}, bf16[16,128,128]{2,1,0:T(8,128)(2,1)}) custom-call(f32[3,1,1,4608]{3,2,1,0:T(1,128)} %get-tuple-element.8.hid, bf16[2,48,128]{2,1,0:T(8,128)(2,1)} %get-tuple-element.9.fresh, bf16[16,128,128]{2,1,0:T(8,128)(2,1)} %bitcast.6, bf16[16,128,128]{2,1,0:T(8,128)(2,1)} %bitcast.8, ...), custom_call_target="tpu_custom_call" | custom-call | tf_op jit(solution)/shard_map/pallas_call | solution.py:746

commit v8 on v6

--- a/solution.py
+++ b/solution.py
@@ -47,11 +47,11 @@
 def kernel(
     dims, prompt_total,
     hid_in, pre_in, post_in, freq_in, perm_in, wq, wk, wv, wout, pk, pv, kc, vc, par_in, lens_in,
-    out_h, out_f,
+    out_h, out_k, out_v,
     hid, pre_gain, post_gain, freq, perm, par, lens,
     tiles, relay, tilesf, cos_rows, sin_rows, a1, a1f, xb, wz, yf, sred, rred, g, gf, qa, kall, vall, acc,
     psend, precv, both, osend, orecv, woutv, kcv, vcv, ancv, freshv, br, csend, crecv, s1, ysend,
-    yrecv, zsend, zrecv,
+    yrecv, zsend, zrecv, freshk, new,
     as_, ar, hs, hr, fs, fr, ws, wr, wzs, wzr, ks, kr, pxs, pxr, pys, pyr, rys, ryr, rxs, rxr, cs, cr, rs, rr, gs,
     gr, qs, qr, ps, pr, os_, or_, bcs, bcr, bys, byr, bzs, bzr, ls,
 ):
@@ -111,6 +111,16 @@
 
     across = at(zl_=(1 - q) * PN + p)
 
+    early = [pltpu.make_async_copy(hid_in, hid, ls.at[6]), pltpu.make_async_copy(pre_in, pre_gain, ls.at[7])]
+    late = [
+        pltpu.make_async_copy(src, dst, ls.at[8 + i])
+        for i, (src, dst) in enumerate(
+            ((post_in, post_gain), (freq_in, freq), (perm_in, perm), (par_in, par), (lens_in, lens))
+        )
+    ]
+    for cp in early:
+        cp.start()
+
     peers = [half_at(m)[0] for m in range(1, GN, 2)]
     peers += [at(zl_=q * PN + p_of(o)) for o in range(1, PN)]
     peers += [at(x_=x_of(o)) for o in range(1, XN)]
@@ -121,15 +131,6 @@
     for peer in peers:
         pl.semaphore_signal(barrier, inc=1, device_id=peer, device_id_type=MESH)
 
-    early = [pltpu.make_async_copy(hid_in, hid, ls.at[6]), pltpu.make_async_copy(pre_in, pre_gain, ls.at[7])]
-    late = [
-        pltpu.make_async_copy(src, dst, ls.at[8 + i])
-        for i, (src, dst) in enumerate(
-            ((post_in, post_gain), (freq_in, freq), (perm_in, perm), (par_in, par), (lens_in, lens))
-        )
-    ]
-    for cp in early + late:
-        cp.start()
     loc = [
         pltpu.make_async_copy(wout, woutv, ls.at[1]),
         pltpu.make_async_copy(kc, kcv, ls.at[2]),
@@ -137,7 +138,7 @@
         pltpu.make_async_copy(pk, kall.at[x], ls.at[4]),
         pltpu.make_async_copy(pv, vall.at[x], ls.at[5]),
     ]
-    for cp in loc:
+    for cp in late + loc:
         cp.start()
 
     J = width // 256
@@ -451,7 +452,6 @@
         cached = jnp.where((anc2 == b) & in_use, cached, 0.0)
         suf_w = suf_w + dot(cached.astype(BF16), vcv[b])
         suf_t = suf_t + jnp.sum(cached, axis=1, keepdims=True)
-    out_f[...] = g[q, 2:4]
 
     for h in range(2):
         both[h] = psend[0, h].astype(F32)
@@ -528,6 +528,20 @@
             kept.append(jnp.where(is_first, total[0:4], total[4:8]))
         else:
             kept.append(total[0:4])
+    at_slot = iota((SLOTS, HEAD), 0)
+    stores = []
+    for i, (cache, dst) in enumerate(((kcv, out_k), (vcv, out_v))):
+        freshk[...] = g[q, 2 + i].astype(F32)
+        for b in range(BEAMS):
+            two = par[2, 0, b]
+            mid = par[1, 0, two]
+            block = cache[par[0, 0, mid]].astype(F32)
+            for u, row in enumerate((mid, two + BEAMS, b + 2 * BEAMS)):
+                block = jnp.where(at_slot == length + u, freshk[pl.ds(row, 1), :], block)
+            new[i, b] = block.astype(BF16)
+        cp = pltpu.make_async_copy(new.at[i], dst, ls.at[13 + i])
+        cp.start()
+        stores.append(cp)
     if ZH > 1:
         for i in range(CHUNKS):
             bz_copies[i].wait_recv()
@@ -542,49 +556,26 @@
 
     for cp in sends:
         cp.wait_send()
+    for cp in stores:
+        cp.wait()
     for to in range(XN):
         @pl.when(x != to)
         def _():
             w_copy(to).wait_send()
 
 
-def cache_kernel(
-    hid, fresh, kc, vc, par, lens, out_h, out_k, out_v, hidv, freshv, old, new, rows, ins, outs, sem
-):
-    beams, slots = kc.shape[0], kc.shape[1]
-    loads = [pltpu.make_async_copy(src, old.at[i], ins.at[i]) for i, src in enumerate((kc, vc))]
-    loads.append(pltpu.make_async_copy(fresh, freshv, ins.at[2]))
-    loads.append(pltpu.make_async_copy(hid, hidv, ins.at[3]))
-    for i in (2, 0, 1, 3):
-        loads[i].start()
-    length = lens[lax.axis_index("context")]
-    window = min(32, slots)
-    start = pl.multiple_of(jnp.minimum(lax.div(length, 16) * 16, slots - window), 16)
-    at_slot = iota((window, HEAD), 0) + start
-    group = max(beams // 4, 1)
-    stores = []
-    loads[2].wait()
-    for i, dst in enumerate((out_k, out_v)):
-        rows[...] = freshv[i].astype(F32)
-        loads[i].wait()
-        for b in range(beams):
-            two = par[2, 0, b]
-            mid = par[1, 0, two]
-            new[i, b] = old[i, par[0, 0, mid]]
-            block = new[i, b, pl.ds(start, window), :].astype(F32)
-            for u, row in enumerate((mid, two + beams, b + 2 * beams)):
-                block = jnp.where(at_slot == length + u, rows[pl.ds(row, 1), :], block)
-            new[i, b, pl.ds(start, window), :] = block.astype(BF16)
-            if (b + 1) % group == 0:
-                span = pl.ds(b + 1 - group, group)
-                cp = pltpu.make_async_copy(new.at[i, span], dst.at[span], outs.at[i, b // group])
-                cp.start()
-                stores.append(cp)
-        if i == 0:
-            loads[3].wait()
-            cp = pltpu.make_async_copy(hidv, out_h, sem)
-            cp.start()
-            stores.append(cp)
+def place_kernel(hid, keys, values, out_h, out_k, out_v, hidv, keysv, valuesv, ins, outs):
+    loads, stores = [], []
+    for i, (src, held, dst) in enumerate(
+        ((keys, keysv, out_k), (values, valuesv, out_v), (hid, hidv, out_h))
+    ):
+        loads.append(pltpu.make_async_copy(src, held, ins.at[i]))
+        stores.append(pltpu.make_async_copy(held, dst, outs.at[i]))
+    for cp in loads:
+        cp.start()
+    for load, store in zip(loads, stores):
+        load.wait()
+        store.start()
     for cp in stores:
         cp.wait()
 
@@ -634,7 +625,6 @@
     perm = jnp.asarray(order_matrix(dims), BF16)
     hbm = pl.BlockSpec(memory_space=pltpu.HBM)
     vmem = pl.BlockSpec(memory_space=pltpu.VMEM)
-    smem = pl.BlockSpec(memory_space=pltpu.SMEM)
     wrows = w_query.shape[0]
     grp = 4 * ZH
     half = YN * grp
@@ -685,6 +675,8 @@
         V((CHUNKS, YN, 2 * grp, wide // 2), BF16),
         V((CHUNKS, 16, wide // 4), BF16),
         V((CHUNKS, 16, wide // 4), BF16),
+        V((rows, HEAD), F32),
+        V((2, beams, slots, HEAD), BF16),
         D((4,)), D((4,)), D((2,)), D((2,)), D((2,)), D((2,)), D((XN,)), D((XN,)), D((PN,)), D((PN,)), D((2, XN, 2)), D((2, XN, 2)),
         D((XN,)), D((XN,)), D((XN, 4)), D((XN, 4)), D((4,)), D((4,)), D((4, XN)), D((4, XN)),
         D((XN, 4)), D((XN, 4)), D((XN,)), D((XN,)), D((XN,)), D((XN,)), D((PN,)), D((PN,)),
@@ -693,14 +685,15 @@
     ]
     keys_in = suffix_key_cache.reshape(beams, slots, HEAD)
     values_in = suffix_value_cache.reshape(beams, slots, HEAD)
-    hidden, fresh = pl.pallas_call(
+    hidden, keys_new, values_new = pl.pallas_call(
         functools.partial(kernel, dims, prompt_total),
         out_shape=(
             jax.ShapeDtypeStruct((STEPS, 1, 1, width), F32),
-            jax.ShapeDtypeStruct((2, rows, HEAD), BF16),
+            jax.ShapeDtypeStruct((beams, slots, HEAD), BF16),
+            jax.ShapeDtypeStruct((beams, slots, HEAD), BF16),
         ),
         in_specs=[hbm] * 15,
-        out_specs=(vmem, vmem),
+        out_specs=(vmem, hbm, hbm),
         scratch_shapes=scratch,
         compiler_params=pltpu.CompilerParams(
             collective_id=0, has_side_effects=True, vmem_limit_bytes=63 * 1024 * 1024
@@ -723,26 +716,23 @@
         lengths,
     )
     hidden_out, keys_out, values_out = pl.pallas_call(
-        cache_kernel,
+        place_kernel,
         out_shape=(
             jax.ShapeDtypeStruct((STEPS, 1, 1, width), F32),
             jax.ShapeDtypeStruct((beams, slots, HEAD), BF16),
             jax.ShapeDtypeStruct((beams, slots, HEAD), BF16),
         ),
-        in_specs=[hbm] * 4 + [smem] * 2,
+        in_specs=[hbm] * 3,
         out_specs=(hbm, hbm, hbm),
         scratch_shapes=[
             V((STEPS, 1, 1, width), F32),
-            V((2, rows, HEAD), BF16),
-            V((2, beams, slots, HEAD), BF16),
-            V((2, beams, slots, HEAD), BF16),
-            V((rows, HEAD), F32),
-            D((4,)),
-            D((2, 4)),
-            D,
+            V((beams, slots, HEAD), BF16),
+            V((beams, slots, HEAD), BF16),
+            D((3,)),
+            D((3,)),
         ],
         compiler_params=pltpu.CompilerParams(vmem_limit_bytes=63 * 1024 * 1024),
-    )(hidden, fresh, keys_in, values_in, parents, lengths)
+    )(hidden, keys_new, values_new)
     return (
         hidden_out,
         keys_out.reshape(1, beams, slots, HEAD),

time: 86.9 us -> 86.1 us (level)
  no operation moved by 1% of the time
where the time goes in v8:
time: 86.1 us; the launch traced here: 85.9 us
  Pallas kernels  85.3 us (99%)
    pallas_call x1, Pallas kernels, body(): pl.pallas_call(functools.partial(kernel, dims, prompt_total), out_shape=(...  83.2 us
    pallas_call x1, Pallas kernels, body(): pl.pallas_call(place_kernel, out_shape=(jax.ShapeDtypeStruct((STEPS, 1, 1...  2.06 us

profile of v8, /device:TPU:1, one launch (start us, length us, event | category | flops | bytes accessed | tf_op | source)
XLA Modules:
  0.0 85.9 jit_solution(10500674658340124150)
XLA Ops:
  0.6 83.2 %shard_map.166 = (f32[3,1,1,4608]{3,2,1,0:T(1,128)}, bf16[16,128,128]{2,1,0:T(8,128)(2,1)}, bf16[16,128,128]{2,1,0:T(8,128)(2,1)}) custom-call(bf16[3,4608]{1,0:T(4,128)(2,1)} %bitcast.7, bf16[4608]{0:T(1024)(128)(2,1)} %pre_in.1, bf16[4608]{0:T(1024)(128)(2,1)} %post_in.1, f32[1,128]{1,0:T(1,128)} %constant.4.clone.freq_in, ...), custom_call_target="tpu_custom_call" | custom-call | tf_op jit(solution)/shard_map/pallas_call | solution.py:688
  83.9 2.1 %shard_map.167 = (f32[3,1,1,4608]{3,2,1,0:T(1,128)}, bf16[16,128,128]{2,1,0:T(8,128)(2,1)}, bf16[16,128,128]{2,1,0:T(8,128)(2,1)}) custom-call(f32[3,1,1,4608]{3,2,1,0:T(1,128)} %get-tuple-element.9.hid, bf16[16,128,128]{2,1,0:T(8,128)(2,1)} %get-tuple-element.10.keys, bf16[16,128,128]{2,1,0:T(8,128)(2,1)} %get-tuple-element.11.values), custom_call_target="tpu_custom_call" | custom-call | tf_op jit(solution)/shard_map/pallas_call | solution.py:718

commit v9 on v8

--- a/solution.py
+++ b/solution.py
@@ -510,6 +510,7 @@
         over_y(i - 1)
     over_y(CHUNKS - 1)
     bz_copies = []
+    before = len(sends)
     kept = []
     is_first = zh == 0
     quarter = wide // 4
@@ -542,6 +543,12 @@
         cp = pltpu.make_async_copy(new.at[i], dst, ls.at[13 + i])
         cp.start()
         stores.append(cp)
+    for cp in sends[:before]:
+        cp.wait_send()
+    for to in range(XN):
+        @pl.when(x != to)
+        def _():
+            w_copy(to).wait_send()
     if ZH > 1:
         for i in range(CHUNKS):
             bz_copies[i].wait_recv()
@@ -554,14 +561,10 @@
     for t in range(STEPS):
         out_h[t, 0] = result[t : t + 1]
 
-    for cp in sends:
+    for cp in sends[before:]:
         cp.wait_send()
     for cp in stores:
         cp.wait()
-    for to in range(XN):
-        @pl.when(x != to)
-        def _():
-            w_copy(to).wait_send()
 
 
 def place_kernel(hid, keys, values, out_h, out_k, out_v, hidv, keysv, valuesv, ins, outs):

time: 86.1 us -> 85.9 us (level)
  no operation moved by 1% of the time
where the time goes in v9:
time: 85.9 us; the launch traced here: 85.8 us
  Pallas kernels  85.1 us (99%)
    pallas_call x1, Pallas kernels, body(): pl.pallas_call(functools.partial(kernel, dims, prompt_total), out_shape=(...  83.1 us
    pallas_call x1, Pallas kernels, body(): pl.pallas_call(place_kernel, out_shape=(jax.ShapeDtypeStruct((STEPS, 1, 1...  2.06 us

profile of v9, /device:TPU:1, one launch (start us, length us, event | category | flops | bytes accessed | tf_op | source)
XLA Modules:
  0.0 85.8 jit_solution(6986709593426828931)
XLA Ops:
  0.6 83.1 %shard_map.166 = (f32[3,1,1,4608]{3,2,1,0:T(1,128)}, bf16[16,128,128]{2,1,0:T(8,128)(2,1)}, bf16[16,128,128]{2,1,0:T(8,128)(2,1)}) custom-call(bf16[3,4608]{1,0:T(4,128)(2,1)} %bitcast.7, bf16[4608]{0:T(1024)(128)(2,1)} %pre_in.1, bf16[4608]{0:T(1024)(128)(2,1)} %post_in.1, f32[1,128]{1,0:T(1,128)} %constant.4.clone.freq_in, ...), custom_call_target="tpu_custom_call" | custom-call | tf_op jit(solution)/shard_map/pallas_call | solution.py:691
  83.7 2.1 %shard_map.167 = (f32[3,1,1,4608]{3,2,1,0:T(1,128)}, bf16[16,128,128]{2,1,0:T(8,128)(2,1)}, bf16[16,128,128]{2,1,0:T(8,128)(2,1)}) custom-call(f32[3,1,1,4608]{3,2,1,0:T(1,128)} %get-tuple-element.9.hid, bf16[16,128,128]{2,1,0:T(8,128)(2,1)} %get-tuple-element.10.keys, bf16[16,128,128]{2,1,0:T(8,128)(2,1)} %get-tuple-element.11.values), custom_call_target="tpu_custom_call" | custom-call | tf_op jit(solution)/shard_map/pallas_call | solution.py:721
